TPU v7x, 32 devices: a whole 2x2x4 slice. The times are simulated.
32 devices in a mesh: row: 4 (over y, x), col: 8 (over z, core).
Axes of the slice: x: 2, y: 2, z: 4, core: 2. Of those that a mesh axis runs over, the one named last changes fastest.
Arguments:
- object_field: float32 [2, 2048, 4096], P(None, 'row', 'col'), may hold values from -5 to 5
- probe: float32 [2, 8, 256, 256], replicated, may hold values from -2.5 to 2.5
- intensity: float32 [64, 256, 256], P(('row', 'col')), may hold values from 0.5 to 4
- row_offset: int32 [64], P(('row', 'col')), may hold values from 0 to 511
- col_offset: int32 [64], P(('row', 'col')), may hold values from 0 to 511
- live: int32 [64], P(('row', 'col')), may hold values 0 or 1
Outputs:
- object_grad: float32 [2, 2048, 4096], P(None, 'row', 'col')
- probe_grad: float32 [2, 8, 256, 256], replicated
All inputs are finite; a program needn't handle non-finite values. No bound on the sum of `live` on one device may be relied on, other than what follows from the above.
Results may differ from a plain program's by a relative error of at most 0.0003.
Values sent between devices are 32-bit elements; how exact they have to be, the bound alone decides.
No kernel may reach another device: no remote copies, remote signals or barrier semaphores. Data moves between devices by JAX's collectives and lax.ppermute only.
A program may use at most 128 MiB of HBM per device.

v0:
```python
import functools

import jax
import jax.numpy as jnp
import ml_dtypes
import numpy as np
from jax import lax
from jax.experimental import pallas as pl
from jax.experimental.pallas import tpu as pltpu
from jax.sharding import PartitionSpec as P

smoothing = 0.25


def passed_along(array, axis, by):
    devices = lax.axis_size(axis)
    pairs = [(i, i + by) for i in range(devices) if 0 <= i + by < devices]
    return lax.ppermute(array, axis, pairs)


def split(x):
    high = x.astype(jnp.bfloat16)
    return high, (x - high.astype(jnp.float32)).astype(jnp.bfloat16)


def matrices(width):
    half = width // 2
    n = np.arange(half)
    scale = 1.0 / np.sqrt(width)
    out = []
    forward_right, forward_left, inverse_left, inverse_right = [], [], [], []
    for parity in (0, 1):
        phase = (n[:, None] * (2 * n[None, :] + parity) % width) * (2.0 * np.pi / width)
        c, s = np.cos(phase) * scale, np.sin(phase) * scale
        forward_right.append(np.block([[c, -s], [s, c]]))
        forward_left.append(np.block([[c.T, s.T], [-s.T, c.T]]))
        inverse_left.append(np.block([[c, -s], [s, c]]))
        inverse_right.append(np.block([[c.T, s.T], [-s.T, c.T]]))
    for pair in (forward_right, forward_left, inverse_left, inverse_right):
        for m in pair:
            high = m.astype(np.float32).astype(ml_dtypes.bfloat16)
            low = (m - high.astype(np.float64)).astype(np.float32).astype(ml_dtypes.bfloat16)
            out += [high, low]
    return np.stack(out)


def dot(a, b):
    return jnp.dot(a, b, preferred_element_type=jnp.float32)


def right(z, mats, at):
    high, low = split(z)
    return dot(high, mats[at]) + (dot(low, mats[at]) + dot(high, mats[at + 1]))


def left(z, mats, at):
    high, low = split(z)
    return dot(mats[at], high) + (dot(mats[at], low) + dot(mats[at + 1], high))


def kernel(
    row_ref, col_ref, live_ref, bit_ref, own, beside, below0, below1, corner, probe, root, mats,
    g_own, g_beside, g_below, g_corner, p_keep, p_send,
    ext, grad, spec, patch, factor, placed, sems,
):
    patterns, width = root.shape[0], root.shape[-1]
    modes = probe.shape[1]
    half = width // 2
    rows, cols = own.shape[1], own.shape[2]
    keep = modes // 2

    def part(e, top, height, left_of, wide):
        return e.at[:, pl.ds(top, height), pl.ds(left_of, wide)]

    arriving = [
        pltpu.make_async_copy(src, dst, sems.at[i])
        for i, (src, dst) in enumerate(
            (
                (own, part(ext, 0, rows, 0, cols)),
                (beside, part(ext, 0, rows, cols, width)),
                (below0, part(ext, rows, width, 0, width)),
                (below1, part(ext, rows, width, width, cols - width)),
                (corner, part(ext, rows, width, cols, width)),
            )
        )
    ]
    for copy in arriving:
        copy.start()
    grad[...] = jnp.zeros_like(grad)
    for copy in arriving:
        copy.wait()

    tall, wide = width + 8, width + 128

    def turned(x, by, axis):
        return pltpu.roll(x, jnp.where(by == 0, 0, x.shape[axis] - by), axis)

    for p in range(patterns):
        top = pl.multiple_of((row_ref[p] // 8) * 8, 8)
        drop = row_ref[p] % 8
        base = pl.multiple_of((col_ref[p] // 128) * 128, 128)
        shift = col_ref[p] % 128
        for c in range(2):
            window = turned(ext[c, pl.ds(top, tall), pl.ds(base, wide)], drop, 0)[:width]
            patch[c] = turned(window, shift, 1)[:, :width]
        factor[...] = jnp.zeros_like(factor)

        def forward(m, carry):
            o_re, o_im = patch[0], patch[1]
            q_re, q_im = probe[0, m], probe[1, m]
            e_re = q_re * o_re - q_im * o_im
            e_im = q_re * o_im + q_im * o_re
            r0, r1 = e_re[:, :half], e_re[:, half:]
            i0, i1 = e_im[:, :half], e_im[:, half:]
            even = right(jnp.concatenate([r0 + r1, i0 + i1], axis=1), mats, 0)
            odd = right(jnp.concatenate([r0 - r1, i0 - i1], axis=1), mats, 2)
            re = jnp.concatenate([even[:, :half], odd[:, :half]], axis=1)
            im = jnp.concatenate([even[:, half:], odd[:, half:]], axis=1)
            f0 = left(jnp.concatenate([re[:half] + re[half:], im[:half] + im[half:]], axis=0), mats, 4)
            f1 = left(jnp.concatenate([re[:half] - re[half:], im[:half] - im[half:]], axis=0), mats, 6)
            spec[m, 0] = f0
            spec[m, 1] = f1
            factor[0] += f0[:half] * f0[:half] + f0[half:] * f0[half:]
            factor[1] += f1[:half] * f1[:half] + f1[half:] * f1[half:]
            return carry

        lax.fori_loop(0, modes, forward, 0)
        alive = live_ref[p].astype(jnp.float32)
        factor[...] = (1.0 - root[p] / jnp.sqrt(factor[...] + smoothing)) * alive
        placed[...] = jnp.zeros_like(placed)

        def backward(out, first, j, carry):
            group = (j // (modes // 4)) % 2
            m = j ^ bit_ref[0] ^ bit_ref[1 + group]
            scale0 = factor[0]
            scale1 = factor[1]
            e = left(spec[m, 0] * jnp.concatenate([scale0, scale0], axis=0), mats, 8)
            o = left(spec[m, 1] * jnp.concatenate([scale1, scale1], axis=0), mats, 10)
            total, other = e + o, e - o
            re = jnp.concatenate([total[:half], other[:half]], axis=0)
            im = jnp.concatenate([total[half:], other[half:]], axis=0)
            even = right(jnp.concatenate([re[:, :half], im[:, :half]], axis=1), mats, 12)
            odd = right(jnp.concatenate([re[:, half:], im[:, half:]], axis=1), mats, 14)
            total, other = even + odd, even - odd
            x_re = jnp.concatenate([total[:, :half], other[:, :half]], axis=1)
            x_im = jnp.concatenate([total[:, half:], other[:, half:]], axis=1)
            q_re, q_im = probe[0, m], probe[1, m]
            placed[0, :width, :width] += q_re * x_re + q_im * x_im
            placed[1, :width, :width] += q_re * x_im - q_im * x_re
            o_re, o_im = patch[0], patch[1]
            gains = (o_re * x_re + o_im * x_im, o_re * x_im - o_im * x_re)
            for c in range(2):
                for h in range(2):
                    down = pl.multiple_of((h ^ bit_ref[5]) * half, half)
                    at = (j - first, c ^ bit_ref[3 + group], pl.ds(down, half))
                    value = gains[c][h * half : (h + 1) * half]
                    if p == 0:
                        out[at] = value
                    else:
                        out[at] = out[at] + value
            return carry

        lax.fori_loop(keep, modes, functools.partial(backward, p_send, keep), 0)
        lax.fori_loop(0, keep, functools.partial(backward, p_keep, 0), 0)
        for c in range(2):
            at = (c, pl.ds(top, tall), pl.ds(base, wide))
            grad[at] = grad[at] + pltpu.roll(pltpu.roll(placed[c], drop, 0), shift, 1)

    leaving = [
        pltpu.make_async_copy(src, dst, sems.at[i])
        for i, (src, dst) in enumerate(
            (
                (part(grad, 0, rows, 0, cols), g_own),
                (part(grad, 0, rows, cols, width), g_beside),
                (part(grad, rows, width, 0, cols), g_below),
                (part(grad, rows, width, cols, width), g_corner),
            )
        )
    ]
    for copy in leaving:
        copy.start()
    for copy in leaving:
        copy.wait()


def parity_order(intensity, orders, root):
    half = root.shape[2]

    def parts(x):
        high, low = split(x)
        return high, low, (x - high.astype(jnp.float32) - low.astype(jnp.float32)).astype(jnp.bfloat16)

    for p in range(root.shape[0]):
        high, middle, low = parts(jnp.sqrt(intensity[p]))
        x = dot(orders[0], high) + dot(orders[0], middle) + dot(orders[0], low)
        high, middle, low = parts(x)
        x = dot(high, orders[1]) + dot(middle, orders[1]) + dot(low, orders[1])
        root[p, 0] = x[:half]
        root[p, 1] = x[half:]


def assemble(bit_ref, *refs):
    pieces, out, sems = refs[:-2], refs[-2], refs[-1]
    modes, width = out.shape[1], out.shape[-1]
    half = width // 2
    each = modes // len(pieces)
    copies = []
    for slot in range(modes):
        piece, inner = divmod(slot, each)
        group = (slot // (modes // 4)) % 2
        m = slot ^ bit_ref[0] ^ bit_ref[1 + group]
        for c in range(2):
            for h in range(2):
                down = pl.multiple_of((h ^ bit_ref[5]) * half, half)
                copies.append(
                    pltpu.make_async_copy(
                        pieces[piece].at[inner, c, pl.ds(h * half, half)],
                        out.at[c ^ bit_ref[3 + group], m, pl.ds(down, half)],
                        sems.at[len(copies)],
                    )
                )
    for copy in copies:
        copy.start()
    for copy in copies:
        copy.wait()


def swap(array, where):
    axis, bit = where
    return lax.ppermute(array, axis, [(i, i ^ (1 << bit)) for i in range(lax.axis_size(axis))])


def bit_of(where):
    axis, bit = where
    return (lax.axis_index(axis) >> bit) & 1


def probe_sum(p_keep, p_send, bits, order):
    core, first, second, third, rest = order
    keep, width = p_keep.shape[0], p_keep.shape[-1]
    one = keep // 4
    half = width // 2
    came = swap(p_send, core)
    a_came = swap(p_keep[one : 2 * one] + came[one : 2 * one], first)
    b_came = swap(p_keep[3 * one :] + came[3 * one :], second)

    def a_of(at):
        return p_keep[:one, at] + came[:one, at] + a_came[:, at]

    def b_of(at):
        return p_keep[2 * one : 3 * one, at] + came[2 * one : 3 * one, at] + b_came[:, at]

    a_more = swap(a_of(1), second)
    b_more = swap(b_of(1), first)
    both = jnp.stack([a_of(0) + a_more, b_of(0) + b_more])
    z_came = swap(both[:, :, half:], third)
    z = both[:, :, :half] + z_came
    for where in rest:
        z = z + swap(z, where)
    z_other = swap(z, third)
    a = jnp.concatenate([z[0], z_other[0]], axis=1)
    b = jnp.concatenate([z[1], z_other[1]], axis=1)
    a = jnp.stack([a, swap(a, second)], axis=1)
    b = jnp.stack([b, swap(b, first)], axis=1)
    pieces = [a, swap(a, first), b, swap(b, second)]
    pieces = pieces + [swap(piece, core) for piece in pieces]
    modes = 2 * keep
    return pl.pallas_call(
        assemble,
        out_shape=jax.ShapeDtypeStruct((2, modes, width, width), jnp.float32),
        in_specs=[pl.BlockSpec(memory_space=pltpu.SMEM)] + [pl.BlockSpec(memory_space=pltpu.VMEM)] * len(pieces),
        out_specs=pl.BlockSpec(memory_space=pl.ANY),
        scratch_shapes=[pltpu.SemaphoreType.DMA((4 * modes,))],
        compiler_params=pltpu.CompilerParams(vmem_limit_bytes=24 * 1024 * 1024),
    )(bits, *pieces)


def shards(object_field, probe, intensity, row_offset, col_offset, live):
    width = probe.shape[-1]
    modes = probe.shape[1]
    patterns = intensity.shape[0]
    half = width // 2
    rows, cols = object_field.shape[1:]
    row_bits = [("row", i) for i in range(lax.axis_size("row").bit_length() - 1)]
    col_bits = [("col", i) for i in range(lax.axis_size("col").bit_length() - 1)]
    core, first, second = col_bits[0], row_bits[0], row_bits[1]
    others = col_bits[1:] + row_bits[2:]
    order = (core, first, second, others[0], others[1:])

    below0 = passed_along(object_field[:, :width, :width], "row", -1)
    below1 = passed_along(object_field[:, :width, width:], "row", -1)
    beside = passed_along(object_field[:, :, :width], "col", -1)
    corner = passed_along(below0, "col", -1)
    smem = pl.BlockSpec(memory_space=pltpu.SMEM)
    vmem = pl.BlockSpec(memory_space=pltpu.VMEM)
    hbm = pl.BlockSpec(memory_space=pl.ANY)
    f32 = jnp.float32
    order_rows = np.eye(width)[np.concatenate([np.arange(0, width, 2), np.arange(1, width, 2)])]
    root = pl.pallas_call(
        parity_order,
        out_shape=jax.ShapeDtypeStruct((patterns, 2, half, width), f32),
        in_specs=[vmem, vmem],
        out_specs=vmem,
    )(intensity, jnp.asarray(np.stack([order_rows, order_rows.T]), jnp.bfloat16))
    bits = jnp.stack(
        [
            bit_of(core) * (modes // 2),
            bit_of(first) * (modes // 8),
            bit_of(second) * (modes // 8),
            bit_of(second),
            bit_of(first),
            bit_of(others[0]),
        ]
    ).astype(jnp.int32)
    mats = jnp.asarray(matrices(width))
    g_own, g_beside, g_below, g_corner, p_keep, p_send = pl.pallas_call(
        kernel,
        out_shape=(
            jax.ShapeDtypeStruct((2, rows, cols), f32),
            jax.ShapeDtypeStruct((2, rows, width), f32),
            jax.ShapeDtypeStruct((2, width, cols), f32),
            jax.ShapeDtypeStruct((2, width, width), f32),
            jax.ShapeDtypeStruct((modes // 2, 2, width, width), f32),
            jax.ShapeDtypeStruct((modes // 2, 2, width, width), f32),
        ),
        in_specs=[smem] * 4 + [hbm] * 5 + [vmem] * 3,
        out_specs=(hbm, hbm, hbm, hbm, vmem, vmem),
        scratch_shapes=[
            pltpu.VMEM((2, rows + width, cols + width), f32),
            pltpu.VMEM((2, rows + width, cols + width), f32),
            pltpu.VMEM((modes, 2, width, width), f32),
            pltpu.VMEM((2, width, width), f32),
            pltpu.VMEM((2, half, width), f32),
            pltpu.VMEM((2, width + 8, width + 128), f32),
            pltpu.SemaphoreType.DMA((5,)),
        ],
        compiler_params=pltpu.CompilerParams(vmem_limit_bytes=48 * 1024 * 1024),
    )(row_offset, col_offset, live, bits, object_field, beside, below0, below1, corner, probe, root, mats)

    probe_grad = probe_sum(p_keep, p_send, bits, order)
    below_grad = g_below.at[:, :, :width].add(passed_along(g_corner, "col", 1))
    from_left = passed_along(g_beside, "col", 1)
    from_above = passed_along(below_grad, "row", 1)
    object_grad = g_own.at[:, :, :width].add(from_left)
    object_grad = object_grad.at[:, :width, :].add(from_above)
    return (object_grad, probe_grad)


def solution(mesh):
    in_specs = (
        P(None, "row", "col"),
        P(),
        P(("row", "col"), None, None),
        P(("row", "col")),
        P(("row", "col")),
        P(("row", "col")),
    )
    out_specs = (P(None, "row", "col"), P())
    return jax.shard_map(shards, mesh=mesh, in_specs=in_specs, out_specs=out_specs, check_vma=False)
```

profile of v0, /device:TPU:0, one launch (start us, length us, event | category | flops | bytes accessed | tf_op | source)
XLA Modules:
  0.0 170.8 jit_solution(14258723342661664385)
XLA Ops:
  0.6 1.5 fusion.13
  2.1 1.4 collective-permute-start.1
  7.2 12.6 %collective-permute-done.1.below0 = f32[2,256,256]{2,1,0:T(8,128)S(1)} collective-permute-done((f32[2,256,256]{2,1,0:T(8,128)S(1)}, f32[2,256,256]{2,1,0:T(8,128)S(1)}, u32[]{:S(2)}, u32[]{:S(2)}) %collective-permute-start.1) | collective-permute-done | bytes 524320 | tf_op jit(solution)/shard_map/ppermute | solution.py:18
  21.2 2.8 %shard_map.95.root = f32[2,2,128,256]{3,2,1,0:T(8,128)} custom-call(f32[2,256,256]{2,1,0:T(8,128)} %intensity.1, bf16[2,256,256]{2,1,0:T(8,128)(2,1)} %constant.89.clone.orders), custom_call_target="tpu_custom_call" | custom-call | tf_op jit(solution)/shard_map/pallas_call | solution.py:299
  24.0 6.2 %collective-permute-done.2.below1 = f32[2,256,256]{2,1,0:T(8,128)S(1)} collective-permute-done((f32[2,256,256]{2,1,0:T(8,128)S(1)}, f32[2,256,256]{2,1,0:T(8,128)S(1)}, u32[]{:S(2)}, u32[]{:S(2)}) %collective-permute-start.2) | collective-permute-done | bytes 524320 | tf_op jit(solution)/shard_map/ppermute | solution.py:18
  31.3 35.9 %shard_map.96 = (f32[2,512,512]{2,1,0:T(8,128)}, f32[2,512,256]{2,1,0:T(8,128)S(1)}, f32[2,256,512]{2,1,0:T(8,128)S(1)}, f32[2,256,256]{2,1,0:T(8,128)S(1)}, f32...) custom-call(s32[2]{0:T(128)S(1)} %copy-done.1, s32[2]{0:T(128)S(1)} %copy-done.2, s32[2]{0:T(128)S(1)} %copy-done.3, ...), custom_call_target="tpu_custom_call" | custom-call | tf_op jit(solution)/shard_map/pallas_call | solution.py:316
  67.9 4.0 %collective-permute-done.7 = f32[4,2,256,256]{3,2,1,0:T(8,128)S(1)} collective-permute-done((f32[4,2,256,256]{3,2,1,0:T(8,128)}, f32[4,2,256,256]{3,2,1,0:T(8,128)S(1)}, u32[]{:S(2)}, u32[]{:S(2)}) %collective-permute-start.7) | collective-permute-done | bytes 2097184 | tf_op jit(solution)/shard_map/ppermute | solution.py:230
  71.9 1.3 slice_add_fusion.2
  73.2 2.5 %collective-permute-start.8 = (f32[1,2,256,256]{3,2,1,0:T(8,128)S(1)}, f32[1,2,256,256]{3,2,1,0:T(8,128)S(1)}, u32[]{:S(2)}, u32[]{:S(2)}) collective-permute-start(f32[1,2,256,256]{3,2,1,0:T(8,128)S(1)} %get-tuple-element.54), channel_id=1, source_target_pairs={{0,8},{8,0},{16,24},{24,16},{1,9},{9,1},{17,25},{25,17},{2,10},{10... | collective-permute-start | bytes 1572872 | tf_op jit(solution)/shard_map/ppermute | solution.py:230
  75.7 12.4 %collective-permute-done.8 = f32[1,2,256,256]{3,2,1,0:T(8,128)S(1)} collective-permute-done((f32[1,2,256,256]{3,2,1,0:T(8,128)S(1)}, f32[1,2,256,256]{3,2,1,0:T(8,128)S(1)}, u32[]{:S(2)}, u32[]{:S(2)}) %collective-permute-start.8) | collective-permute-done | bytes 524320 | tf_op jit(solution)/shard_map/ppermute | solution.py:230
  88.1 1.5 collective-permute-done.10
  90.9 6.3 %collective-permute-done.9 = f32[1,256,256]{2,1,0:T(8,128)S(1)} collective-permute-done((f32[1,256,256]{2,1,0:T(8,128)S(1)}, f32[1,256,256]{2,1,0:T(8,128)S(1)}, u32[]{:S(2)}, u32[]{:S(2)}) %collective-permute-start.9) | collective-permute-done | bytes 262176 | tf_op jit(solution)/shard_map/ppermute | solution.py:230
  97.7 1.7 collective-permute-start.12
  99.3 5.0 %collective-permute-done.12 = f32[2,1,128,256]{3,2,1,0:T(8,128)S(1)} collective-permute-done((f32[2,1,128,256]{3,2,1,0:T(8,128)S(1)}, f32[2,1,128,256]{3,2,1,0:T(8,128)S(1)}, u32[]{:S(2)}, u32[]{:S(2)}) %collective-permute-start.12) | collective-permute-done | bytes 262176 | tf_op jit(solution)/shard_map/ppermute | solution.py:230
  104.3 2.7 %collective-permute-start.13 = (f32[2,1,128,256]{3,2,1,0:T(8,128)S(1)}, f32[2,1,128,256]{3,2,1,0:T(8,128)S(1)}, u32[]{:S(2)}, u32[]{:S(2)}) collective-permute-start(f32[2,1,128,256]{3,2,1,0:T(8,128)S(1)} %fusion.2), channel_id=1, source_target_pairs={{0,4},{1,5},{2,6},{3,7},{4,0},{5,1},{6,2},{7,3},{8,12},{9,13},{10,... | collective-permute-start | bytes 786440 | tf_op jit(solution)/shard_map/ppermute | solution.py:230
  107.0 9.5 %collective-permute-done.13 = f32[2,1,128,256]{3,2,1,0:T(8,128)S(1)} collective-permute-done((f32[2,1,128,256]{3,2,1,0:T(8,128)S(1)}, f32[2,1,128,256]{3,2,1,0:T(8,128)S(1)}, u32[]{:S(2)}, u32[]{:S(2)}) %collective-permute-start.13) | collective-permute-done | bytes 262176 | tf_op jit(solution)/shard_map/ppermute | solution.py:230
  118.0 4.7 %collective-permute-start.4 = (f32[2,512,256]{2,1,0:T(8,128)S(1)}, f32[2,512,256]{2,1,0:T(8,128)S(1)}, u32[]{:S(2)}, u32[]{:S(2)}) collective-permute-start(f32[2,512,256]{2,1,0:T(8,128)S(1)} %get-tuple-element.45), channel_id=1, source_target_pairs={{0,1},{1,2},{2,3},{3,4},{4,5},{5,6},{6,7},{8,9},{9,10},{10,11},{11... | collective-permute-start | bytes 3145736 | tf_op jit(solution)/shard_map/ppermute | solution.py:18
  124.8 1.4 collective-permute-start.15
  126.3 2.2 %collective-permute-start.6 = (f32[2,256,512]{2,1,0:T(8,128)S(1)}, f32[2,256,512]{2,1,0:T(8,128)S(1)}, u32[]{:S(2)}, u32[]{:S(2)}) collective-permute-start(f32[2,256,512]{2,1,0:T(8,128)S(1)} %add_dynamic-update-slice_fusion.1), channel_id=1, source_target_pairs={{0,8},{8,16},{16,24},{1,9},{9,17},{17,25},{2,10},{10,18},{18,26},{... | collective-permute-start | bytes 3145736 | tf_op jit(solution)/shard_map/ppermute | solution.py:18
  128.5 3.1 %collective-permute-done.15 = f32[1,256,256]{2,1,0:T(8,128)S(1)} collective-permute-done((f32[1,256,256]{2,1,0:T(8,128)S(1)}, f32[1,256,256]{2,1,0:T(8,128)S(1)}, u32[]{:S(2)}, u32[]{:S(2)}) %collective-permute-start.15) | collective-permute-done | bytes 262176 | tf_op jit(solution)/shard_map/ppermute | solution.py:230
  131.7 1.3 collective-permute-start.16
  133.8 4.8 %collective-permute-start.21 = (f32[1,2,256,256]{3,2,1,0:T(8,128)S(1)}, f32[1,2,256,256]{3,2,1,0:T(8,128)S(1)}, u32[]{:S(2)}, u32[]{:S(2)}) collective-permute-start(f32[1,2,256,256]{3,2,1,0:T(8,128)S(1)} %pad_maximum_fusion.1.refs_2_), channel_id=1, source_target_pairs={{0,1},{1,0},{2,3},{3,2},{4,5},{5,4},{6,7},{7,6},{8,9},{9,8},{10,11... | collective-permute-start | bytes 1572872 | tf_op jit(solution)/shard_map/ppermute | solution.py:230
  138.6 26.8 %collective-permute-done.16.refs_1_ = f32[1,2,256,256]{3,2,1,0:T(8,128)S(1)} collective-permute-done((f32[1,2,256,256]{3,2,1,0:T(8,128)S(1)}, f32[1,2,256,256]{3,2,1,0:T(8,128)S(1)}, u32[]{:S(2)}, u32[]{:S(2)}) %collective-permute-start.16) | collective-permute-done | bytes 524320 | tf_op jit(solution)/shard_map/ppermute | solution.py:230
  168.0 2.8 %shard_map.97 = f32[2,8,256,256]{3,2,1,0:T(8,128)} custom-call(s32[6]{0:T(128)S(1)} %stack.48.bit_ref, f32[1,2,256,256]{3,2,1,0:T(8,128)S(1)} %pad_maximum_fusion.refs_0_, f32[1,2,256,256]{3,2,1,0:T(8,128)S(1)} %collective-permute-done.16.refs_1_, f32[1,2,256,256]{3,2,1,0:T(8,128)S(1)} %pad_maximum_fusion.1.refs_2_, ...), custom_call_target="tpu_custom_call" | custom-call | tf_op jit(solution)/shard_map/pallas_call | solution.py:268
  (59 shorter events, 15.6 us)
Async XLA Ops:
  2.1 17.7 %collective-permute-start.1 = (f32[2,256,256]{2,1,0:T(8,128)S(1)}, f32[2,256,256]{2,1,0:T(8,128)S(1)}, u32[]{:S(2)}, u32[]{:S(2)}) collective-permute-start(f32[2,256,256]{2,1,0:T(8,128)S(1)} %get-tuple-element.57), channel_id=1, source_target_pairs={{8,0},{16,8},{24,16},{9,1},{17,9},{25,17},{10,2},{18,10},{26,18},{... | collective-permute-start | bytes 1572872 | tf_op jit(solution)/shard_map/ppermute | solution.py:18
  4.7 25.6 %collective-permute-start = (f32[2,512,256]{2,1,0:T(8,128)}, f32[2,512,256]{2,1,0:T(8,128)S(1)}, u32[]{:S(2)}, u32[]{:S(2)}) collective-permute-start(f32[2,512,256]{2,1,0:T(8,128)} %slice.147), channel_id=1, source_target_pairs={{1,0},{2,1},{3,2},{4,3},{5,4},{6,5},{7,6},{9,8},{10,9},{11,10},{12... | collective-permute-start | bytes 3145736 | tf_op jit(solution)/shard_map/ppermute | solution.py:18
  5.9 24.3 %collective-permute-start.2 = (f32[2,256,256]{2,1,0:T(8,128)S(1)}, f32[2,256,256]{2,1,0:T(8,128)S(1)}, u32[]{:S(2)}, u32[]{:S(2)}) collective-permute-start(f32[2,256,256]{2,1,0:T(8,128)S(1)} %get-tuple-element.56), channel_id=1, source_target_pairs={{8,0},{16,8},{24,16},{9,1},{17,9},{25,17},{10,2},{18,10},{26,18},{... | collective-permute-start | bytes 1572872 | tf_op jit(solution)/shard_map/ppermute | solution.py:18
  19.9 10.4 %collective-permute-start.3 = (f32[2,256,256]{2,1,0:T(8,128)S(1)}, f32[2,256,256]{2,1,0:T(8,128)S(1)}, u32[]{:S(2)}, u32[]{:S(2)}) collective-permute-start(f32[2,256,256]{2,1,0:T(8,128)S(1)} %collective-permute-done.1.below0), channel_id=1, source_target_pairs={{1,0},{2,1},{3,2},{4,3},{5,4},{6,5},{7,6},{9,8},{10,9},{11,10},{12... | collective-permute-start | bytes 1572872 | tf_op jit(solution)/shard_map/ppermute | solution.py:18
  67.2 4.7 %collective-permute-start.7 = (f32[4,2,256,256]{3,2,1,0:T(8,128)}, f32[4,2,256,256]{3,2,1,0:T(8,128)S(1)}, u32[]{:S(2)}, u32[]{:S(2)}) collective-permute-start(f32[4,2,256,256]{3,2,1,0:T(8,128)} %get-tuple-element.49), channel_id=1, source_target_pairs={{0,1},{1,0},{2,3},{3,2},{4,5},{5,4},{6,7},{7,6},{8,9},{9,8},{10,11... | collective-permute-start | bytes 6291464 | tf_op jit(solution)/shard_map/ppermute | solution.py:230
  73.2 14.9 %collective-permute-start.8 = (f32[1,2,256,256]{3,2,1,0:T(8,128)S(1)}, f32[1,2,256,256]{3,2,1,0:T(8,128)S(1)}, u32[]{:S(2)}, u32[]{:S(2)}) collective-permute-start(f32[1,2,256,256]{3,2,1,0:T(8,128)S(1)} %get-tuple-element.54), channel_id=1, source_target_pairs={{0,8},{8,0},{16,24},{24,16},{1,9},{9,1},{17,25},{25,17},{2,10},{10... | collective-permute-start | bytes 1572872 | tf_op jit(solution)/shard_map/ppermute | solution.py:230
  75.7 13.9 %collective-permute-start.10 = (f32[1,2,256,256]{3,2,1,0:T(8,128)S(1)}, f32[1,2,256,256]{3,2,1,0:T(8,128)S(1)}, u32[]{:S(2)}, u32[]{:S(2)}) collective-permute-start(f32[1,2,256,256]{3,2,1,0:T(8,128)S(1)} %get-tuple-element.55), channel_id=1, source_target_pairs={{0,16},{8,24},{16,0},{24,8},{1,17},{9,25},{17,1},{25,9},{2,18},{10... | collective-permute-start | bytes 1572872 | tf_op jit(solution)/shard_map/ppermute | solution.py:230
  89.7 7.5 %collective-permute-start.9 = (f32[1,256,256]{2,1,0:T(8,128)S(1)}, f32[1,256,256]{2,1,0:T(8,128)S(1)}, u32[]{:S(2)}, u32[]{:S(2)}) collective-permute-start(f32[1,256,256]{2,1,0:T(8,128)S(1)} %get-tuple-element.52), channel_id=1, source_target_pairs={{0,16},{8,24},{16,0},{24,8},{1,17},{9,25},{17,1},{25,9},{2,18},{10... | collective-permute-start | bytes 786440 | tf_op jit(solution)/shard_map/ppermute | solution.py:230
  90.0 7.5 %collective-permute-start.11 = (f32[1,256,256]{2,1,0:T(8,128)S(1)}, f32[1,256,256]{2,1,0:T(8,128)S(1)}, u32[]{:S(2)}, u32[]{:S(2)}) collective-permute-start(f32[1,256,256]{2,1,0:T(8,128)S(1)} %get-tuple-element.53), channel_id=1, source_target_pairs={{0,8},{8,0},{16,24},{24,16},{1,9},{9,1},{17,25},{25,17},{2,10},{10... | collective-permute-start | bytes 786440 | tf_op jit(solution)/shard_map/ppermute | solution.py:230
  97.7 6.6 %collective-permute-start.12 = (f32[2,1,128,256]{3,2,1,0:T(8,128)S(1)}, f32[2,1,128,256]{3,2,1,0:T(8,128)S(1)}, u32[]{:S(2)}, u32[]{:S(2)}) collective-permute-start(f32[2,1,128,256]{3,2,1,0:T(8,128)S(1)} %pad_maximum_fusion.2), channel_id=1, source_target_pairs={{0,2},{1,3},{2,0},{3,1},{4,6},{5,7},{6,4},{7,5},{8,10},{9,11},{10,... | collective-permute-start | bytes 786440 | tf_op jit(solution)/shard_map/ppermute | solution.py:230
  104.3 12.2 %collective-permute-start.13 = (f32[2,1,128,256]{3,2,1,0:T(8,128)S(1)}, f32[2,1,128,256]{3,2,1,0:T(8,128)S(1)}, u32[]{:S(2)}, u32[]{:S(2)}) collective-permute-start(f32[2,1,128,256]{3,2,1,0:T(8,128)S(1)} %fusion.2), channel_id=1, source_target_pairs={{0,4},{1,5},{2,6},{3,7},{4,0},{5,1},{6,2},{7,3},{8,12},{9,13},{10,... | collective-permute-start | bytes 786440 | tf_op jit(solution)/shard_map/ppermute | solution.py:230
  116.6 7.2 %collective-permute-start.14 = (f32[2,1,128,256]{3,2,1,0:T(8,128)S(1)}, f32[2,1,128,256]{3,2,1,0:T(8,128)S(1)}, u32[]{:S(2)}, u32[]{:S(2)}) collective-permute-start(f32[2,1,128,256]{3,2,1,0:T(8,128)S(1)} %fusion.14), channel_id=1, source_target_pairs={{0,2},{1,3},{2,0},{3,1},{4,6},{5,7},{6,4},{7,5},{8,10},{9,11},{10,... | collective-permute-start | bytes 786440 | tf_op jit(solution)/shard_map/ppermute | solution.py:230
  116.7 9.5 %collective-permute-start.5 = (f32[2,256,256]{2,1,0:T(8,128)S(1)}, f32[2,256,256]{2,1,0:T(8,128)S(1)}, u32[]{:S(2)}, u32[]{:S(2)}) collective-permute-start(f32[2,256,256]{2,1,0:T(8,128)S(1)} %get-tuple-element.47), channel_id=1, source_target_pairs={{0,1},{1,2},{2,3},{3,4},{4,5},{5,6},{6,7},{8,9},{9,10},{10,11},{11... | collective-permute-start | bytes 1572872 | tf_op jit(solution)/shard_map/ppermute | solution.py:18
  118.0 15.8 %collective-permute-start.4 = (f32[2,512,256]{2,1,0:T(8,128)S(1)}, f32[2,512,256]{2,1,0:T(8,128)S(1)}, u32[]{:S(2)}, u32[]{:S(2)}) collective-permute-start(f32[2,512,256]{2,1,0:T(8,128)S(1)} %get-tuple-element.45), channel_id=1, source_target_pairs={{0,1},{1,2},{2,3},{3,4},{4,5},{5,6},{6,7},{8,9},{9,10},{10,11},{11... | collective-permute-start | bytes 3145736 | tf_op jit(solution)/shard_map/ppermute | solution.py:18
  123.9 9.1 %collective-permute-start.17 = (f32[1,256,256]{2,1,0:T(8,128)S(1)}, f32[1,256,256]{2,1,0:T(8,128)S(1)}, u32[]{:S(2)}, u32[]{:S(2)}) collective-permute-start(f32[1,256,256]{2,1,0:T(8,128)S(1)} %get-tuple-element.59), channel_id=1, source_target_pairs={{0,8},{8,0},{16,24},{24,16},{1,9},{9,1},{17,25},{25,17},{2,10},{10... | collective-permute-start | bytes 786440 | tf_op jit(solution)/shard_map/ppermute | solution.py:230
  124.7 41.1 %copy-start.5 = (f32[2,512,512]{2,1,0:T(8,128)S(1)}, f32[2,512,512]{2,1,0:T(8,128)}, u32[]{:S(2)}) copy-start(f32[2,512,512]{2,1,0:T(8,128)} %get-tuple-element.44) | copy-start | bytes 6291460
  124.8 6.9 %collective-permute-start.15 = (f32[1,256,256]{2,1,0:T(8,128)S(1)}, f32[1,256,256]{2,1,0:T(8,128)S(1)}, u32[]{:S(2)}, u32[]{:S(2)}) collective-permute-start(f32[1,256,256]{2,1,0:T(8,128)S(1)} %get-tuple-element.65), channel_id=1, source_target_pairs={{0,16},{8,24},{16,0},{24,8},{1,17},{9,25},{17,1},{25,9},{2,18},{10... | collective-permute-start | bytes 786440 | tf_op jit(solution)/shard_map/ppermute | solution.py:230
  126.3 39.8 %collective-permute-start.6 = (f32[2,256,512]{2,1,0:T(8,128)S(1)}, f32[2,256,512]{2,1,0:T(8,128)S(1)}, u32[]{:S(2)}, u32[]{:S(2)}) collective-permute-start(f32[2,256,512]{2,1,0:T(8,128)S(1)} %add_dynamic-update-slice_fusion.1), channel_id=1, source_target_pairs={{0,8},{8,16},{16,24},{1,9},{9,17},{17,25},{2,10},{10,18},{18,26},{... | collective-permute-start | bytes 3145736 | tf_op jit(solution)/shard_map/ppermute | solution.py:18
  131.7 33.7 %collective-permute-start.16 = (f32[1,2,256,256]{3,2,1,0:T(8,128)S(1)}, f32[1,2,256,256]{3,2,1,0:T(8,128)S(1)}, u32[]{:S(2)}, u32[]{:S(2)}) collective-permute-start(f32[1,2,256,256]{3,2,1,0:T(8,128)S(1)} %pad_maximum_fusion.refs_0_), channel_id=1, source_target_pairs={{0,8},{8,0},{16,24},{24,16},{1,9},{9,1},{17,25},{25,17},{2,10},{10... | collective-permute-start | bytes 1572872 | tf_op jit(solution)/shard_map/ppermute | solution.py:230
  133.0 32.3 %collective-permute-start.18 = (f32[1,2,256,256]{3,2,1,0:T(8,128)S(1)}, f32[1,2,256,256]{3,2,1,0:T(8,128)S(1)}, u32[]{:S(2)}, u32[]{:S(2)}) collective-permute-start(f32[1,2,256,256]{3,2,1,0:T(8,128)S(1)} %pad_maximum_fusion.1.refs_2_), channel_id=1, source_target_pairs={{0,16},{8,24},{16,0},{24,8},{1,17},{9,25},{17,1},{25,9},{2,18},{10... | collective-permute-start | bytes 1572872 | tf_op jit(solution)/shard_map/ppermute | solution.py:230
  133.8 32.6 %collective-permute-start.19 = (f32[1,2,256,256]{3,2,1,0:T(8,128)S(1)}, f32[1,2,256,256]{3,2,1,0:T(8,128)S(1)}, u32[]{:S(2)}, u32[]{:S(2)}) collective-permute-start(f32[1,2,256,256]{3,2,1,0:T(8,128)S(1)} %pad_maximum_fusion.refs_0_), channel_id=1, source_target_pairs={{0,1},{1,0},{2,3},{3,2},{4,5},{5,4},{6,7},{7,6},{8,9},{9,8},{10,11... | collective-permute-start | bytes 1572872 | tf_op jit(solution)/shard_map/ppermute | solution.py:230
  133.8 32.6 %collective-permute-start.21 = (f32[1,2,256,256]{3,2,1,0:T(8,128)S(1)}, f32[1,2,256,256]{3,2,1,0:T(8,128)S(1)}, u32[]{:S(2)}, u32[]{:S(2)}) collective-permute-start(f32[1,2,256,256]{3,2,1,0:T(8,128)S(1)} %pad_maximum_fusion.1.refs_2_), channel_id=1, source_target_pairs={{0,1},{1,0},{2,3},{3,2},{4,5},{5,4},{6,7},{7,6},{8,9},{9,8},{10,11... | collective-permute-start | bytes 1572872 | tf_op jit(solution)/shard_map/ppermute | solution.py:230
  165.3 1.9 %collective-permute-start.20 = (f32[1,2,256,256]{3,2,1,0:T(8,128)S(1)}, f32[1,2,256,256]{3,2,1,0:T(8,128)S(1)}, u32[]{:S(2)}, u32[]{:S(2)}) collective-permute-start(f32[1,2,256,256]{3,2,1,0:T(8,128)S(1)} %collective-permute-done.16.refs_1_), channel_id=1, source_target_pairs={{0,1},{1,0},{2,3},{3,2},{4,5},{5,4},{6,7},{7,6},{8,9},{9,8},{10,11... | collective-permute-start | bytes 1572872 | tf_op jit(solution)/shard_map/ppermute | solution.py:230
  165.3 2.7 %collective-permute-start.22 = (f32[1,2,256,256]{3,2,1,0:T(8,128)S(1)}, f32[1,2,256,256]{3,2,1,0:T(8,128)S(1)}, u32[]{:S(2)}, u32[]{:S(2)}) collective-permute-start(f32[1,2,256,256]{3,2,1,0:T(8,128)S(1)} %collective-permute-done.18.refs_3_), channel_id=1, source_target_pairs={{0,1},{1,0},{2,3},{3,2},{4,5},{5,4},{6,7},{7,6},{8,9},{9,8},{10,11... | collective-permute-start | bytes 1572872 | tf_op jit(solution)/shard_map/ppermute | solution.py:230
  (7 other events, 115.3 us)
where the time goes:
time: 171 us
  waiting for transfers between devices  90.4 us (53%)
  Pallas kernels  41.5 us (24%)
  starting transfers between devices  31.8 us (19%)
  local copies, waits for them, and re-layouts  3.73 us (2%)
  other arithmetic  2.5 us (1%)
    ppermute x16, waiting for transfers between devices, swap(): lax.ppermute(array, axis, [(i, i ^ 1 << bit) for i in range(lax.axis_size...  71.5 us
    pallas_call x1, Pallas kernels, shards(): pl.pallas_call(kernel, out_shape=(jax.ShapeDtypeStruct((2, rows, cols), f...  35.9 us
    ppermute x7, waiting for transfers between devices, passed_along(): return lax.ppermute(array, axis, pairs)  18.9 us
    ppermute x16, starting transfers between devices, swap(): lax.ppermute(array, axis, [(i, i ^ 1 << bit) for i in range(lax.axis_size...  18.4 us
    ppermute x7, starting transfers between devices, passed_along(): return lax.ppermute(array, axis, pairs)  13.5 us
  transfers between devices with their start and end apart: 23, of which 14 were waited for; matrix products, arithmetic and copies ran while one was open for 1% of the time, Pallas kernels for 2%

commit v1 on v0

--- a/solution.py
+++ b/solution.py
@@ -60,7 +60,7 @@
 
 def kernel(
     row_ref, col_ref, live_ref, bit_ref, own, beside, below0, below1, corner, probe, root, mats,
-    g_own, g_beside, g_below, g_corner, p_keep, p_send,
+    g_own, g_beside, g_below, g_corner, keep0, keep1, send0, send1,
     ext, grad, spec, patch, factor, placed, sems,
 ):
     patterns, width = root.shape[0], root.shape[-1]
@@ -130,7 +130,7 @@
         placed[...] = jnp.zeros_like(placed)
 
         def backward(out, first, j, carry):
-            group = (j // (modes // 4)) % 2
+            group = first // keep
             m = j ^ bit_ref[0] ^ bit_ref[1 + group]
             scale0 = factor[0]
             scale1 = factor[1]
@@ -160,8 +160,9 @@
                         out[at] = out[at] + value
             return carry
 
-        lax.fori_loop(keep, modes, functools.partial(backward, p_send, keep), 0)
-        lax.fori_loop(0, keep, functools.partial(backward, p_keep, 0), 0)
+        quarter = modes // 4
+        for first, out in ((keep, send0), (0, keep0), (keep + quarter, send1), (quarter, keep1)):
+            lax.fori_loop(first, first + quarter, functools.partial(backward, out, first), 0)
         for c in range(2):
             at = (c, pl.ds(top, tall), pl.ds(base, wide))
             grad[at] = grad[at] + pltpu.roll(pltpu.roll(placed[c], drop, 0), shift, 1)
@@ -207,7 +208,7 @@
     copies = []
     for slot in range(modes):
         piece, inner = divmod(slot, each)
-        group = (slot // (modes // 4)) % 2
+        group = slot // (modes // 2)
         m = slot ^ bit_ref[0] ^ bit_ref[1 + group]
         for c in range(2):
             for h in range(2):
@@ -235,37 +236,44 @@
     return (lax.axis_index(axis) >> bit) & 1
 
 
-def probe_sum(p_keep, p_send, bits, order):
-    core, first, second, third, rest = order
-    keep, width = p_keep.shape[0], p_keep.shape[-1]
-    one = keep // 4
-    half = width // 2
-    came = swap(p_send, core)
-    a_came = swap(p_keep[one : 2 * one] + came[one : 2 * one], first)
-    b_came = swap(p_keep[3 * one :] + came[3 * one :], second)
-
-    def a_of(at):
-        return p_keep[:one, at] + came[:one, at] + a_came[:, at]
-
-    def b_of(at):
-        return p_keep[2 * one : 3 * one, at] + came[2 * one : 3 * one, at] + b_came[:, at]
-
-    a_more = swap(a_of(1), second)
-    b_more = swap(b_of(1), first)
-    both = jnp.stack([a_of(0) + a_more, b_of(0) + b_more])
-    z_came = swap(both[:, :, half:], third)
-    z = both[:, :, :half] + z_came
-    for where in rest:
-        z = z + swap(z, where)
-    z_other = swap(z, third)
-    a = jnp.concatenate([z[0], z_other[0]], axis=1)
-    b = jnp.concatenate([z[1], z_other[1]], axis=1)
-    a = jnp.stack([a, swap(a, second)], axis=1)
-    b = jnp.stack([b, swap(b, first)], axis=1)
-    pieces = [a, swap(a, first), b, swap(b, second)]
-    pieces = pieces + [swap(piece, core) for piece in pieces]
-    modes = 2 * keep
-    return pl.pallas_call(
+def after(array, earlier):
+    return array + 0.0 * earlier.reshape(-1)[0]
+
+
+def hop(array, turn):
+    n_row, n_col = lax.axis_size("row"), lax.axis_size("col")
+    pairs = []
+    for r in range(n_row):
+        for c in range(n_col):
+            pairs.append((r * n_col + c, (r ^ (1 << ((turn + c) % 2))) * n_col + c))
+    return lax.ppermute(array, ("row", "col"), pairs)
+
+
+def probe_sum(kept, sent, bits, core, third, rest, below_grad):
+    one = kept[0].shape[0] // 2
+    half = kept[0].shape[-1] // 2
+    totals = []
+    for keep, send in zip(kept, sent):
+        came = swap(send, core)
+        came1 = hop(keep[one:] + came[one:], 0)
+        came2 = hop(keep[:one, 1] + came[:one, 1] + came1[:, 1], 1)
+        below_grad = after(below_grad, came2)
+        totals.append(keep[:one, 0] + came[:one, 0] + came1[:, 0] + came2)
+    from_above = passed_along(below_grad, "row", 1)
+    own = []
+    for number, total in enumerate(totals):
+        total = total[:, :half] + swap(total[:, half:], third)
+        for where in rest:
+            total = total + swap(total, where)
+        total = jnp.concatenate([total, swap(total, third)], axis=1)
+        if number == 1:
+            total = after(total, from_above)
+        total = jnp.stack([total, hop(total, 1)], axis=1)
+        own += [total, hop(total, 0)]
+    pieces = own + [swap(piece, core) for piece in own]
+    modes = 4 * kept[0].shape[0]
+    width = kept[0].shape[-1]
+    probe_grad = pl.pallas_call(
         assemble,
         out_shape=jax.ShapeDtypeStruct((2, modes, width, width), jnp.float32),
         in_specs=[pl.BlockSpec(memory_space=pltpu.SMEM)] + [pl.BlockSpec(memory_space=pltpu.VMEM)] * len(pieces),
@@ -273,6 +281,7 @@
         scratch_shapes=[pltpu.SemaphoreType.DMA((4 * modes,))],
         compiler_params=pltpu.CompilerParams(vmem_limit_bytes=24 * 1024 * 1024),
     )(bits, *pieces)
+    return probe_grad, from_above
 
 
 def shards(object_field, probe, intensity, row_offset, col_offset, live):
@@ -283,9 +292,8 @@
     rows, cols = object_field.shape[1:]
     row_bits = [("row", i) for i in range(lax.axis_size("row").bit_length() - 1)]
     col_bits = [("col", i) for i in range(lax.axis_size("col").bit_length() - 1)]
-    core, first, second = col_bits[0], row_bits[0], row_bits[1]
+    core, x_bit, y_bit = col_bits[0], row_bits[0], row_bits[1]
     others = col_bits[1:] + row_bits[2:]
-    order = (core, first, second, others[0], others[1:])
 
     below0 = passed_along(object_field[:, :width, :width], "row", -1)
     below1 = passed_along(object_field[:, :width, width:], "row", -1)
@@ -302,29 +310,25 @@
         in_specs=[vmem, vmem],
         out_specs=vmem,
     )(intensity, jnp.asarray(np.stack([order_rows, order_rows.T]), jnp.bfloat16))
+    side, x, y = bit_of(core), bit_of(x_bit), bit_of(y_bit)
+    kept_first = jnp.where(side == 0, x, y)
+    kept_second = jnp.where(side == 0, y, x)
+    eighth = modes // 8
     bits = jnp.stack(
-        [
-            bit_of(core) * (modes // 2),
-            bit_of(first) * (modes // 8),
-            bit_of(second) * (modes // 8),
-            bit_of(second),
-            bit_of(first),
-            bit_of(others[0]),
-        ]
+        [side * (modes // 2), kept_first * eighth, kept_second * eighth, kept_second, kept_first, bit_of(others[0])]
     ).astype(jnp.int32)
     mats = jnp.asarray(matrices(width))
-    g_own, g_beside, g_below, g_corner, p_keep, p_send = pl.pallas_call(
+    g_own, g_beside, g_below, g_corner, keep0, keep1, send0, send1 = pl.pallas_call(
         kernel,
         out_shape=(
             jax.ShapeDtypeStruct((2, rows, cols), f32),
             jax.ShapeDtypeStruct((2, rows, width), f32),
             jax.ShapeDtypeStruct((2, width, cols), f32),
             jax.ShapeDtypeStruct((2, width, width), f32),
-            jax.ShapeDtypeStruct((modes // 2, 2, width, width), f32),
-            jax.ShapeDtypeStruct((modes // 2, 2, width, width), f32),
+            *[jax.ShapeDtypeStruct((modes // 4, 2, width, width), f32)] * 4,
         ),
         in_specs=[smem] * 4 + [hbm] * 5 + [vmem] * 3,
-        out_specs=(hbm, hbm, hbm, hbm, vmem, vmem),
+        out_specs=(*[hbm] * 4, *[vmem] * 4),
         scratch_shapes=[
             pltpu.VMEM((2, rows + width, cols + width), f32),
             pltpu.VMEM((2, rows + width, cols + width), f32),
@@ -337,10 +341,11 @@
         compiler_params=pltpu.CompilerParams(vmem_limit_bytes=48 * 1024 * 1024),
     )(row_offset, col_offset, live, bits, object_field, beside, below0, below1, corner, probe, root, mats)
 
-    probe_grad = probe_sum(p_keep, p_send, bits, order)
     below_grad = g_below.at[:, :, :width].add(passed_along(g_corner, "col", 1))
     from_left = passed_along(g_beside, "col", 1)
-    from_above = passed_along(below_grad, "row", 1)
+    probe_grad, from_above = probe_sum(
+        (keep0, keep1), (send0, send1), bits, core, others[0], others[1:], below_grad
+    )
     object_grad = g_own.at[:, :, :width].add(from_left)
     object_grad = object_grad.at[:, :width, :].add(from_above)
     return (object_grad, probe_grad)

time: 171 us -> 151 us (0.88)
  waiting for transfers between devices: 90.4 us -> 57.8 us
  starting transfers between devices: 31.8 us -> 38.8 us
  local copies, waits for them, and re-layouts: 3.73 us -> 6.75 us
  between operations: 0.93 us -> 3.13 us
    ppermute x16 -> x12, waiting for transfers between devices: 71.5 us -> 7.1 us  [swap(): lax.ppermute(array, axis, [(i, i ^ 1 << bit) for i in range(lax.axis_size...]
    ppermute x0 -> x8, waiting for transfers between devices: none -> 26.4 us  [hop(): return lax.ppermute(array, ('row', 'col'), pairs)]
    ppermute x0 -> x8, starting transfers between devices: none -> 11.7 us  [hop(): return lax.ppermute(array, ('row', 'col'), pairs)]
    ppermute x7, waiting for transfers between devices: 18.9 us -> 24.3 us  [passed_along(): return lax.ppermute(array, axis, pairs)]
    ppermute x16 -> x12, starting transfers between devices: 18.4 us -> 15 us  [swap(): lax.ppermute(array, axis, [(i, i ^ 1 << bit) for i in range(lax.axis_size...]
  transfers between devices with their start and end apart: 23 -> 27, of which waited for: 14 -> 13; matrix products, arithmetic and copies ran while one was open for 1% -> 4% of each run, Pallas kernels for 2% -> 2%
where the time goes in v1:
time: 151 us; the launch traced here: 150 us
  waiting for transfers between devices  57.8 us (38%)
  Pallas kernels  41.1 us (27%)
  starting transfers between devices  38.8 us (26%)
  local copies, waits for them, and re-layouts  6.75 us (4%)
  between operations  3.13 us (2%)
  other arithmetic  2.46 us (2%)
    pallas_call x1, Pallas kernels, shards(): pl.pallas_call(kernel, out_shape=(jax.ShapeDtypeStruct((2, rows, cols), f...  35.5 us
    ppermute x8, waiting for transfers between devices, hop(): return lax.ppermute(array, ('row', 'col'), pairs)  26.4 us
    ppermute x7, waiting for transfers between devices, passed_along(): return lax.ppermute(array, axis, pairs)  24.3 us
    ppermute x12, starting transfers between devices, swap(): lax.ppermute(array, axis, [(i, i ^ 1 << bit) for i in range(lax.axis_size...  15 us
    ppermute x7, starting transfers between devices, passed_along(): return lax.ppermute(array, axis, pairs)  12.1 us
    ppermute x8, starting transfers between devices, hop(): return lax.ppermute(array, ('row', 'col'), pairs)  11.7 us
    ppermute x12, waiting for transfers between devices, swap(): lax.ppermute(array, axis, [(i, i ^ 1 << bit) for i in range(lax.axis_size...  7.1 us
  transfers between devices with their start and end apart: 27, of which 13 were waited for; matrix products, arithmetic and copies ran while one was open for 4% of the time, Pallas kernels for 2%

profile of v1, /device:TPU:0, one launch (start us, length us, event | category | flops | bytes accessed | tf_op | source)
XLA Modules:
  0.0 150.0 jit_solution(4182993984590611980)
XLA Ops:
  0.6 1.5 fusion.8
  7.2 12.6 %collective-permute-done.1.below0 = f32[2,256,256]{2,1,0:T(8,128)S(1)} collective-permute-done((f32[2,256,256]{2,1,0:T(8,128)S(1)}, f32[2,256,256]{2,1,0:T(8,128)S(1)}, u32[]{:S(2)}, u32[]{:S(2)}) %collective-permute-start.1) | collective-permute-done | bytes 524320 | tf_op jit(solution)/shard_map/ppermute | solution.py:18
  21.2 2.8 %shard_map.95.root = f32[2,2,128,256]{3,2,1,0:T(8,128)} custom-call(f32[2,256,256]{2,1,0:T(8,128)} %intensity.1, bf16[2,256,256]{2,1,0:T(8,128)(2,1)} %constant.94.clone.orders), custom_call_target="tpu_custom_call" | custom-call | tf_op jit(solution)/shard_map/pallas_call | solution.py:307
  24.1 6.2 %collective-permute-done.2.below1 = f32[2,256,256]{2,1,0:T(8,128)S(1)} collective-permute-done((f32[2,256,256]{2,1,0:T(8,128)S(1)}, f32[2,256,256]{2,1,0:T(8,128)S(1)}, u32[]{:S(2)}, u32[]{:S(2)}) %collective-permute-start.2) | collective-permute-done | bytes 524320 | tf_op jit(solution)/shard_map/ppermute | solution.py:18
  32.3 35.5 %shard_map.96 = (f32[2,512,512]{2,1,0:T(8,128)}, f32[2,512,256]{2,1,0:T(8,128)S(1)}, f32[2,256,512]{2,1,0:T(8,128)S(1)}, f32[2,256,256]{2,1,0:T(8,128)S(1)}, f32...) custom-call(s32[2]{0:T(128)S(1)} %copy-done.1, ...), custom_call_target="tpu_custom_call" | custom-call | tf_op jit(solution)/shard_map/pallas_call | solution.py:321
  68.5 2.4 %collective-permute-done.6 = f32[2,2,256,256]{3,2,1,0:T(8,128)S(1)} collective-permute-done((f32[2,2,256,256]{3,2,1,0:T(8,128)}, f32[2,2,256,256]{3,2,1,0:T(8,128)S(1)}, u32[]{:S(2)}, u32[]{:S(2)}) %collective-permute-start.6) | collective-permute-done | bytes 1048608 | tf_op jit(solution)/shard_map/ppermute | solution.py:231
  71.0 2.5 %collective-permute-start.7 = (f32[1,2,256,256]{3,2,1,0:T(8,128)S(1)}, f32[1,2,256,256]{3,2,1,0:T(8,128)S(1)}, u32[]{:S(2)}, u32[]{:S(2)}) collective-permute-start(f32[1,2,256,256]{3,2,1,0:T(8,128)S(1)} %slice_add_fusion.2), channel_id=1, source_target_pairs={{0,8},{1,17},{2,10},{3,19},{4,12},{5,21},{6,14},{7,23},{8,0},{9,25... | collective-permute-start | bytes 1572872 | tf_op jit(solution)/shard_map/ppermute | solution.py:249
  77.3 3.3 %collective-permute-done.7 = f32[1,2,256,256]{3,2,1,0:T(8,128)S(1)} collective-permute-done((f32[1,2,256,256]{3,2,1,0:T(8,128)S(1)}, f32[1,2,256,256]{3,2,1,0:T(8,128)S(1)}, u32[]{:S(2)}, u32[]{:S(2)}) %collective-permute-start.7) | collective-permute-done | bytes 524320 | tf_op jit(solution)/shard_map/ppermute | solution.py:249
  81.9 7.1 %collective-permute-done.10 = f32[1,2,256,256]{3,2,1,0:T(8,128)S(1)} collective-permute-done((f32[1,2,256,256]{3,2,1,0:T(8,128)S(1)}, f32[1,2,256,256]{3,2,1,0:T(8,128)S(1)}, u32[]{:S(2)}, u32[]{:S(2)}) %collective-permute-start.10) | collective-permute-done | bytes 524320 | tf_op jit(solution)/shard_map/ppermute | solution.py:249
  91.3 1.6 %collective-permute-start.13 = (f32[1,128,256]{2,1,0:T(8,128)S(1)}, f32[1,128,256]{2,1,0:T(8,128)S(1)}, u32[]{:S(2)}, u32[]{:S(2)}) collective-permute-start(f32[1,128,256]{2,1,0:T(8,128)S(1)} %slice.191), channel_id=1, source_target_pairs={{0,2},{1,3},{2,0},{3,1},{4,6},{5,7},{6,4},{7,5},{8,10},{9,11},{10,... | collective-permute-start | bytes 393224 | tf_op jit(solution)/shard_map/ppermute | solution.py:231
  92.9 2.7 %collective-permute-done.11 = f32[1,256,256]{2,1,0:T(8,128)S(1)} collective-permute-done((f32[1,256,256]{2,1,0:T(8,128)S(1)}, f32[1,256,256]{2,1,0:T(8,128)S(1)}, u32[]{:S(2)}, u32[]{:S(2)}) %collective-permute-start.11) | collective-permute-done | bytes 262176 | tf_op jit(solution)/shard_map/ppermute | solution.py:249
  97.6 4.2 %collective-permute-start.12 = (f32[2,256,512]{2,1,0:T(8,128)S(1)}, f32[2,256,512]{2,1,0:T(8,128)S(1)}, u32[]{:S(2)}, u32[]{:S(2)}) collective-permute-start(f32[2,256,512]{2,1,0:T(8,128)S(1)} %add_add_fusion), channel_id=1, source_target_pairs={{0,8},{8,16},{16,24},{1,9},{9,17},{17,25},{2,10},{10,18},{18,26},{... | collective-permute-start | bytes 3145736 | tf_op jit(solution)/shard_map/ppermute | solution.py:18
  101.9 1.6 %collective-permute-start.18 = (f32[1,128,256]{2,1,0:T(8,128)S(1)}, f32[1,128,256]{2,1,0:T(8,128)S(1)}, u32[]{:S(2)}, u32[]{:S(2)}) collective-permute-start(f32[1,128,256]{2,1,0:T(8,128)S(1)} %slice.195), channel_id=1, source_target_pairs={{0,2},{1,3},{2,0},{3,1},{4,6},{5,7},{6,4},{7,5},{8,10},{9,11},{10,... | collective-permute-start | bytes 393224 | tf_op jit(solution)/shard_map/ppermute | solution.py:231
  103.5 2.7 %collective-permute-start.14 = (f32[1,128,256]{2,1,0:T(8,128)S(1)}, f32[1,128,256]{2,1,0:T(8,128)S(1)}, u32[]{:S(2)}, u32[]{:S(2)}) collective-permute-start(f32[1,128,256]{2,1,0:T(8,128)S(1)} %slice_add_fusion.12), channel_id=1, source_target_pairs={{0,4},{1,5},{2,6},{3,7},{4,0},{5,1},{6,2},{7,3},{8,12},{9,13},{10,... | collective-permute-start | bytes 393224 | tf_op jit(solution)/shard_map/ppermute | solution.py:231
  106.2 2.0 %collective-permute-done.18 = f32[1,128,256]{2,1,0:T(8,128)S(1)} collective-permute-done((f32[1,128,256]{2,1,0:T(8,128)S(1)}, f32[1,128,256]{2,1,0:T(8,128)S(1)}, u32[]{:S(2)}, u32[]{:S(2)}) %collective-permute-start.18) | collective-permute-done | bytes 131104 | tf_op jit(solution)/shard_map/ppermute | solution.py:231
  108.3 2.4 %collective-permute-start.19 = (f32[1,128,256]{2,1,0:T(8,128)S(1)}, f32[1,128,256]{2,1,0:T(8,128)S(1)}, u32[]{:S(2)}, u32[]{:S(2)}) collective-permute-start(f32[1,128,256]{2,1,0:T(8,128)S(1)} %slice_add_fusion.11), channel_id=1, source_target_pairs={{0,4},{1,5},{2,6},{3,7},{4,0},{5,1},{6,2},{7,3},{8,12},{9,13},{10,... | collective-permute-start | bytes 393224 | tf_op jit(solution)/shard_map/ppermute | solution.py:231
  110.8 2.4 %collective-permute-start.15 = (f32[1,128,256]{2,1,0:T(8,128)S(1)}, f32[1,128,256]{2,1,0:T(8,128)S(1)}, u32[]{:S(2)}, u32[]{:S(2)}) collective-permute-start(f32[1,128,256]{2,1,0:T(8,128)S(1)} %add.206), channel_id=1, source_target_pairs={{0,2},{1,3},{2,0},{3,1},{4,6},{5,7},{6,4},{7,5},{8,10},{9,11},{10,... | collective-permute-start | bytes 393224 | tf_op jit(solution)/shard_map/ppermute | solution.py:231
  114.4 3.1 %collective-permute-start.20 = (f32[1,128,256]{2,1,0:T(8,128)S(1)}, f32[1,128,256]{2,1,0:T(8,128)S(1)}, u32[]{:S(2)}, u32[]{:S(2)}) collective-permute-start(f32[1,128,256]{2,1,0:T(8,128)S(1)} %add.212), channel_id=1, source_target_pairs={{0,2},{1,3},{2,0},{3,1},{4,6},{5,7},{6,4},{7,5},{8,10},{9,11},{10,... | collective-permute-start | bytes 393224 | tf_op jit(solution)/shard_map/ppermute | solution.py:231
  119.0 5.4 %collective-permute-done.12 = f32[2,256,512]{2,1,0:T(8,128)S(1)} collective-permute-done((f32[2,256,512]{2,1,0:T(8,128)S(1)}, f32[2,256,512]{2,1,0:T(8,128)S(1)}, u32[]{:S(2)}, u32[]{:S(2)}) %collective-permute-start.12) | collective-permute-done | bytes 1048608 | tf_op jit(solution)/shard_map/ppermute | solution.py:18
  126.0 1.9 %collective-permute-start.21 = (f32[1,256,256]{2,1,0:T(8,128)S(1)}, f32[1,256,256]{2,1,0:T(8,128)S(1)}, u32[]{:S(2)}, u32[]{:S(2)}) collective-permute-start(f32[1,256,256]{2,1,0:T(8,128)S(1)} %maximum_add_fusion.1), channel_id=1, source_target_pairs={{0,16},{1,9},{2,18},{3,11},{4,20},{5,13},{6,22},{7,15},{8,24},{9,1... | collective-permute-start | bytes 786440 | tf_op jit(solution)/shard_map/ppermute | solution.py:249
  128.7 6.6 %collective-permute-done.21 = f32[1,256,256]{2,1,0:T(8,128)S(1)} collective-permute-done((f32[1,256,256]{2,1,0:T(8,128)S(1)}, f32[1,256,256]{2,1,0:T(8,128)S(1)}, u32[]{:S(2)}, u32[]{:S(2)}) %collective-permute-start.21) | collective-permute-done | bytes 262176 | tf_op jit(solution)/shard_map/ppermute | solution.py:249
  135.4 2.5 %collective-permute-start.22 = (f32[1,2,256,256]{3,2,1,0:T(8,128)S(1)}, f32[1,2,256,256]{3,2,1,0:T(8,128)S(1)}, u32[]{:S(2)}, u32[]{:S(2)}) collective-permute-start(f32[1,2,256,256]{3,2,1,0:T(8,128)S(1)} %pad_maximum_fusion.1.refs_2_), channel_id=1, source_target_pairs={{0,8},{1,17},{2,10},{3,19},{4,12},{5,21},{6,14},{7,23},{8,0},{9,25... | collective-permute-start | bytes 1572872 | tf_op jit(solution)/shard_map/ppermute | solution.py:249
  138.4 6.6 %collective-permute-done.22.refs_3_ = f32[1,2,256,256]{3,2,1,0:T(8,128)S(1)} collective-permute-done((f32[1,2,256,256]{3,2,1,0:T(8,128)S(1)}, f32[1,2,256,256]{3,2,1,0:T(8,128)S(1)}, u32[]{:S(2)}, u32[]{:S(2)}) %collective-permute-start.22) | collective-permute-done | bytes 524320 | tf_op jit(solution)/shard_map/ppermute | solution.py:249
  147.0 2.8 %shard_map.97 = f32[2,8,256,256]{3,2,1,0:T(8,128)} custom-call(s32[6]{0:T(128)S(1)} %stack.37.bit_ref, f32[1,2,256,256]{3,2,1,0:T(8,128)S(1)} %pad_maximum_fusion.refs_0_, f32[1,2,256,256]{3,2,1,0:T(8,128)S(1)} %collective-permute-done.17.refs_1_, f32[1,2,256,256]{3,2,1,0:T(8,128)S(1)} %pad_maximum_fusion.1.refs_2_, ...), custom_call_target="tpu_custom_call" | custom-call | tf_op jit(solution)/shard_map/pallas_call | solution.py:276
  (81 shorter events, 24.3 us)
Async XLA Ops:
  2.1 17.7 %collective-permute-start.1 = (f32[2,256,256]{2,1,0:T(8,128)S(1)}, f32[2,256,256]{2,1,0:T(8,128)S(1)}, u32[]{:S(2)}, u32[]{:S(2)}) collective-permute-start(f32[2,256,256]{2,1,0:T(8,128)S(1)} %get-tuple-element.55), channel_id=1, source_target_pairs={{8,0},{16,8},{24,16},{9,1},{17,9},{25,17},{10,2},{18,10},{26,18},{... | collective-permute-start | bytes 1572872 | tf_op jit(solution)/shard_map/ppermute | solution.py:18
  4.7 25.6 %collective-permute-start = (f32[2,512,256]{2,1,0:T(8,128)}, f32[2,512,256]{2,1,0:T(8,128)S(1)}, u32[]{:S(2)}, u32[]{:S(2)}) collective-permute-start(f32[2,512,256]{2,1,0:T(8,128)} %slice.150), channel_id=1, source_target_pairs={{1,0},{2,1},{3,2},{4,3},{5,4},{6,5},{7,6},{9,8},{10,9},{11,10},{12... | collective-permute-start | bytes 3145736 | tf_op jit(solution)/shard_map/ppermute | solution.py:18
  5.9 24.3 %collective-permute-start.2 = (f32[2,256,256]{2,1,0:T(8,128)S(1)}, f32[2,256,256]{2,1,0:T(8,128)S(1)}, u32[]{:S(2)}, u32[]{:S(2)}) collective-permute-start(f32[2,256,256]{2,1,0:T(8,128)S(1)} %get-tuple-element.54), channel_id=1, source_target_pairs={{8,0},{16,8},{24,16},{9,1},{17,9},{25,17},{10,2},{18,10},{26,18},{... | collective-permute-start | bytes 1572872 | tf_op jit(solution)/shard_map/ppermute | solution.py:18
  19.9 10.4 %collective-permute-start.3 = (f32[2,256,256]{2,1,0:T(8,128)S(1)}, f32[2,256,256]{2,1,0:T(8,128)S(1)}, u32[]{:S(2)}, u32[]{:S(2)}) collective-permute-start(f32[2,256,256]{2,1,0:T(8,128)S(1)} %collective-permute-done.1.below0), channel_id=1, source_target_pairs={{1,0},{2,1},{3,2},{4,3},{5,4},{6,5},{7,6},{9,8},{10,9},{11,10},{12... | collective-permute-start | bytes 1572872 | tf_op jit(solution)/shard_map/ppermute | solution.py:18
  71.0 9.7 %collective-permute-start.7 = (f32[1,2,256,256]{3,2,1,0:T(8,128)S(1)}, f32[1,2,256,256]{3,2,1,0:T(8,128)S(1)}, u32[]{:S(2)}, u32[]{:S(2)}) collective-permute-start(f32[1,2,256,256]{3,2,1,0:T(8,128)S(1)} %slice_add_fusion.2), channel_id=1, source_target_pairs={{0,8},{1,17},{2,10},{3,19},{4,12},{5,21},{6,14},{7,23},{8,0},{9,25... | collective-permute-start | bytes 1572872 | tf_op jit(solution)/shard_map/ppermute | solution.py:249
  74.6 14.5 %collective-permute-start.10 = (f32[1,2,256,256]{3,2,1,0:T(8,128)S(1)}, f32[1,2,256,256]{3,2,1,0:T(8,128)S(1)}, u32[]{:S(2)}, u32[]{:S(2)}) collective-permute-start(f32[1,2,256,256]{3,2,1,0:T(8,128)S(1)} %slice_add_fusion.1), channel_id=1, source_target_pairs={{0,8},{1,17},{2,10},{3,19},{4,12},{5,21},{6,14},{7,23},{8,0},{9,25... | collective-permute-start | bytes 1572872 | tf_op jit(solution)/shard_map/ppermute | solution.py:249
  76.0 14.4 %collective-permute-start.5 = (f32[2,256,256]{2,1,0:T(8,128)S(1)}, f32[2,256,256]{2,1,0:T(8,128)S(1)}, u32[]{:S(2)}, u32[]{:S(2)}) collective-permute-start(f32[2,256,256]{2,1,0:T(8,128)S(1)} %get-tuple-element.49), channel_id=1, source_target_pairs={{0,1},{1,2},{2,3},{3,4},{4,5},{5,6},{6,7},{8,9},{9,10},{10,11},{11... | collective-permute-start | bytes 1572872 | tf_op jit(solution)/shard_map/ppermute | solution.py:18
  80.7 9.8 %collective-permute-start.8 = (f32[1,256,256]{2,1,0:T(8,128)S(1)}, f32[1,256,256]{2,1,0:T(8,128)S(1)}, u32[]{:S(2)}, u32[]{:S(2)}) collective-permute-start(f32[1,256,256]{2,1,0:T(8,128)S(1)} %fusion.6), channel_id=1, source_target_pairs={{0,16},{1,9},{2,18},{3,11},{4,20},{5,13},{6,22},{7,15},{8,24},{9,1... | collective-permute-start | bytes 786440 | tf_op jit(solution)/shard_map/ppermute | solution.py:249
  89.1 6.4 %collective-permute-start.11 = (f32[1,256,256]{2,1,0:T(8,128)S(1)}, f32[1,256,256]{2,1,0:T(8,128)S(1)}, u32[]{:S(2)}, u32[]{:S(2)}) collective-permute-start(f32[1,256,256]{2,1,0:T(8,128)S(1)} %fusion.5), channel_id=1, source_target_pairs={{0,16},{1,9},{2,18},{3,11},{4,20},{5,13},{6,22},{7,15},{8,24},{9,1... | collective-permute-start | bytes 786440 | tf_op jit(solution)/shard_map/ppermute | solution.py:249
  91.3 12.2 %collective-permute-start.13 = (f32[1,128,256]{2,1,0:T(8,128)S(1)}, f32[1,128,256]{2,1,0:T(8,128)S(1)}, u32[]{:S(2)}, u32[]{:S(2)}) collective-permute-start(f32[1,128,256]{2,1,0:T(8,128)S(1)} %slice.191), channel_id=1, source_target_pairs={{0,2},{1,3},{2,0},{3,1},{4,6},{5,7},{6,4},{7,5},{8,10},{9,11},{10,... | collective-permute-start | bytes 393224 | tf_op jit(solution)/shard_map/ppermute | solution.py:231
  97.6 26.8 %collective-permute-start.12 = (f32[2,256,512]{2,1,0:T(8,128)S(1)}, f32[2,256,512]{2,1,0:T(8,128)S(1)}, u32[]{:S(2)}, u32[]{:S(2)}) collective-permute-start(f32[2,256,512]{2,1,0:T(8,128)S(1)} %add_add_fusion), channel_id=1, source_target_pairs={{0,8},{8,16},{16,24},{1,9},{9,17},{17,25},{2,10},{10,18},{18,26},{... | collective-permute-start | bytes 3145736 | tf_op jit(solution)/shard_map/ppermute | solution.py:18
  101.9 6.4 %collective-permute-start.18 = (f32[1,128,256]{2,1,0:T(8,128)S(1)}, f32[1,128,256]{2,1,0:T(8,128)S(1)}, u32[]{:S(2)}, u32[]{:S(2)}) collective-permute-start(f32[1,128,256]{2,1,0:T(8,128)S(1)} %slice.195), channel_id=1, source_target_pairs={{0,2},{1,3},{2,0},{3,1},{4,6},{5,7},{6,4},{7,5},{8,10},{9,11},{10,... | collective-permute-start | bytes 393224 | tf_op jit(solution)/shard_map/ppermute | solution.py:231
  103.5 7.2 %collective-permute-start.14 = (f32[1,128,256]{2,1,0:T(8,128)S(1)}, f32[1,128,256]{2,1,0:T(8,128)S(1)}, u32[]{:S(2)}, u32[]{:S(2)}) collective-permute-start(f32[1,128,256]{2,1,0:T(8,128)S(1)} %slice_add_fusion.12), channel_id=1, source_target_pairs={{0,4},{1,5},{2,6},{3,7},{4,0},{5,1},{6,2},{7,3},{8,12},{9,13},{10,... | collective-permute-start | bytes 393224 | tf_op jit(solution)/shard_map/ppermute | solution.py:231
  108.3 6.1 %collective-permute-start.19 = (f32[1,128,256]{2,1,0:T(8,128)S(1)}, f32[1,128,256]{2,1,0:T(8,128)S(1)}, u32[]{:S(2)}, u32[]{:S(2)}) collective-permute-start(f32[1,128,256]{2,1,0:T(8,128)S(1)} %slice_add_fusion.11), channel_id=1, source_target_pairs={{0,4},{1,5},{2,6},{3,7},{4,0},{5,1},{6,2},{7,3},{8,12},{9,13},{10,... | collective-permute-start | bytes 393224 | tf_op jit(solution)/shard_map/ppermute | solution.py:231
  110.8 6.7 %collective-permute-start.15 = (f32[1,128,256]{2,1,0:T(8,128)S(1)}, f32[1,128,256]{2,1,0:T(8,128)S(1)}, u32[]{:S(2)}, u32[]{:S(2)}) collective-permute-start(f32[1,128,256]{2,1,0:T(8,128)S(1)} %add.206), channel_id=1, source_target_pairs={{0,2},{1,3},{2,0},{3,1},{4,6},{5,7},{6,4},{7,5},{8,10},{9,11},{10,... | collective-permute-start | bytes 393224 | tf_op jit(solution)/shard_map/ppermute | solution.py:231
  114.4 11.6 %collective-permute-start.20 = (f32[1,128,256]{2,1,0:T(8,128)S(1)}, f32[1,128,256]{2,1,0:T(8,128)S(1)}, u32[]{:S(2)}, u32[]{:S(2)}) collective-permute-start(f32[1,128,256]{2,1,0:T(8,128)S(1)} %add.212), channel_id=1, source_target_pairs={{0,2},{1,3},{2,0},{3,1},{4,6},{5,7},{6,4},{7,5},{8,10},{9,11},{10,... | collective-permute-start | bytes 393224 | tf_op jit(solution)/shard_map/ppermute | solution.py:231
  117.5 10.4 %collective-permute-start.16 = (f32[1,256,256]{2,1,0:T(8,128)S(1)}, f32[1,256,256]{2,1,0:T(8,128)S(1)}, u32[]{:S(2)}, u32[]{:S(2)}) collective-permute-start(f32[1,256,256]{2,1,0:T(8,128)S(1)} %get-tuple-element.57), channel_id=1, source_target_pairs={{0,16},{1,9},{2,18},{3,11},{4,20},{5,13},{6,22},{7,15},{8,24},{9,1... | collective-permute-start | bytes 786440 | tf_op jit(solution)/shard_map/ppermute | solution.py:249
  117.6 27.5 %collective-permute-start.4 = (f32[2,512,256]{2,1,0:T(8,128)S(1)}, f32[2,512,256]{2,1,0:T(8,128)S(1)}, u32[]{:S(2)}, u32[]{:S(2)}) collective-permute-start(f32[2,512,256]{2,1,0:T(8,128)S(1)} %get-tuple-element.47), channel_id=1, source_target_pairs={{0,1},{1,2},{2,3},{3,4},{4,5},{5,6},{6,7},{8,9},{9,10},{10,11},{11... | collective-permute-start | bytes 3145736 | tf_op jit(solution)/shard_map/ppermute | solution.py:18
  126.0 9.3 %collective-permute-start.21 = (f32[1,256,256]{2,1,0:T(8,128)S(1)}, f32[1,256,256]{2,1,0:T(8,128)S(1)}, u32[]{:S(2)}, u32[]{:S(2)}) collective-permute-start(f32[1,256,256]{2,1,0:T(8,128)S(1)} %maximum_add_fusion.1), channel_id=1, source_target_pairs={{0,16},{1,9},{2,18},{3,11},{4,20},{5,13},{6,22},{7,15},{8,24},{9,1... | collective-permute-start | bytes 786440 | tf_op jit(solution)/shard_map/ppermute | solution.py:249
  128.0 10.0 %collective-permute-start.17 = (f32[1,2,256,256]{3,2,1,0:T(8,128)S(1)}, f32[1,2,256,256]{3,2,1,0:T(8,128)S(1)}, u32[]{:S(2)}, u32[]{:S(2)}) collective-permute-start(f32[1,2,256,256]{3,2,1,0:T(8,128)S(1)} %pad_maximum_fusion.refs_0_), channel_id=1, source_target_pairs={{0,8},{1,17},{2,10},{3,19},{4,12},{5,21},{6,14},{7,23},{8,0},{9,25... | collective-permute-start | bytes 1572872 | tf_op jit(solution)/shard_map/ppermute | solution.py:249
  135.4 9.7 %collective-permute-start.22 = (f32[1,2,256,256]{3,2,1,0:T(8,128)S(1)}, f32[1,2,256,256]{3,2,1,0:T(8,128)S(1)}, u32[]{:S(2)}, u32[]{:S(2)}) collective-permute-start(f32[1,2,256,256]{3,2,1,0:T(8,128)S(1)} %pad_maximum_fusion.1.refs_2_), channel_id=1, source_target_pairs={{0,8},{1,17},{2,10},{3,19},{4,12},{5,21},{6,14},{7,23},{8,0},{9,25... | collective-permute-start | bytes 1572872 | tf_op jit(solution)/shard_map/ppermute | solution.py:249
  137.9 7.8 %collective-permute-start.23 = (f32[1,2,256,256]{3,2,1,0:T(8,128)S(1)}, f32[1,2,256,256]{3,2,1,0:T(8,128)S(1)}, u32[]{:S(2)}, u32[]{:S(2)}) collective-permute-start(f32[1,2,256,256]{3,2,1,0:T(8,128)S(1)} %pad_maximum_fusion.refs_0_), channel_id=1, source_target_pairs={{0,1},{1,0},{2,3},{3,2},{4,5},{5,4},{6,7},{7,6},{8,9},{9,8},{10,11... | collective-permute-start | bytes 1572872 | tf_op jit(solution)/shard_map/ppermute | solution.py:231
  137.9 7.8 %collective-permute-start.24 = (f32[1,2,256,256]{3,2,1,0:T(8,128)S(1)}, f32[1,2,256,256]{3,2,1,0:T(8,128)S(1)}, u32[]{:S(2)}, u32[]{:S(2)}) collective-permute-start(f32[1,2,256,256]{3,2,1,0:T(8,128)S(1)} %collective-permute-done.17.refs_1_), channel_id=1, source_target_pairs={{0,1},{1,0},{2,3},{3,2},{4,5},{5,4},{6,7},{7,6},{8,9},{9,8},{10,11... | collective-permute-start | bytes 1572872 | tf_op jit(solution)/shard_map/ppermute | solution.py:231
  138.4 7.3 %collective-permute-start.25 = (f32[1,2,256,256]{3,2,1,0:T(8,128)S(1)}, f32[1,2,256,256]{3,2,1,0:T(8,128)S(1)}, u32[]{:S(2)}, u32[]{:S(2)}) collective-permute-start(f32[1,2,256,256]{3,2,1,0:T(8,128)S(1)} %pad_maximum_fusion.1.refs_2_), channel_id=1, source_target_pairs={{0,1},{1,0},{2,3},{3,2},{4,5},{5,4},{6,7},{7,6},{8,9},{9,8},{10,11... | collective-permute-start | bytes 1572872 | tf_op jit(solution)/shard_map/ppermute | solution.py:231
  (12 other events, 145.2 us)

commit v2 on v1

--- a/solution.py
+++ b/solution.py
@@ -40,8 +40,10 @@
         for m in pair:
             high = m.astype(np.float32).astype(ml_dtypes.bfloat16)
             low = (m - high.astype(np.float64)).astype(np.float32).astype(ml_dtypes.bfloat16)
-            out += [high, low]
-    return np.stack(out)
+            out.append((high, low))
+    rights = [np.concatenate([high, high, low], axis=0) for high, low in out[:2] + out[6:]]
+    lefts = [np.concatenate([high, high, low], axis=1) for high, low in out[2:6]]
+    return np.stack(rights), np.stack(lefts)
 
 
 def dot(a, b):
@@ -50,19 +52,20 @@
 
 def right(z, mats, at):
     high, low = split(z)
-    return dot(high, mats[at]) + (dot(low, mats[at]) + dot(high, mats[at + 1]))
+    return dot(jnp.concatenate([high, low, high], axis=1), mats[0][at // 2 if at < 4 else at // 2 - 4])
 
 
 def left(z, mats, at):
     high, low = split(z)
-    return dot(mats[at], high) + (dot(mats[at], low) + dot(mats[at + 1], high))
+    return dot(mats[1][at // 2 - 2], jnp.concatenate([high, low, high], axis=0))
 
 
 def kernel(
-    row_ref, col_ref, live_ref, bit_ref, own, beside, below0, below1, corner, probe, root, mats,
+    row_ref, col_ref, live_ref, bit_ref, own, beside, below0, below1, corner, probe, root, rights, lefts,
     g_own, g_beside, g_below, g_corner, keep0, keep1, send0, send1,
     ext, grad, spec, patch, factor, placed, sems,
 ):
+    mats = (rights, lefts)
     patterns, width = root.shape[0], root.shape[-1]
     modes = probe.shape[1]
     half = width // 2
@@ -95,19 +98,22 @@
     def turned(x, by, axis):
         return pltpu.roll(x, jnp.where(by == 0, 0, x.shape[axis] - by), axis)
 
+    corners = []
     for p in range(patterns):
         top = pl.multiple_of((row_ref[p] // 8) * 8, 8)
         drop = row_ref[p] % 8
         base = pl.multiple_of((col_ref[p] // 128) * 128, 128)
         shift = col_ref[p] % 128
+        corners.append((top, drop, base, shift))
         for c in range(2):
             window = turned(ext[c, pl.ds(top, tall), pl.ds(base, wide)], drop, 0)[:width]
-            patch[c] = turned(window, shift, 1)[:, :width]
-        factor[...] = jnp.zeros_like(factor)
-
-        def forward(m, carry):
-            o_re, o_im = patch[0], patch[1]
-            q_re, q_im = probe[0, m], probe[1, m]
+            patch[p, c] = turned(window, shift, 1)[:, :width]
+    factor[...] = jnp.zeros_like(factor)
+
+    def forward(m, carry):
+        q_re, q_im = probe[0, m], probe[1, m]
+        for p in range(patterns):
+            o_re, o_im = patch[p, 0], patch[p, 1]
             e_re = q_re * o_re - q_im * o_im
             e_im = q_re * o_im + q_im * o_re
             r0, r1 = e_re[:, :half], e_re[:, half:]
@@ -118,24 +124,27 @@
             im = jnp.concatenate([even[:, half:], odd[:, half:]], axis=1)
             f0 = left(jnp.concatenate([re[:half] + re[half:], im[:half] + im[half:]], axis=0), mats, 4)
             f1 = left(jnp.concatenate([re[:half] - re[half:], im[:half] - im[half:]], axis=0), mats, 6)
-            spec[m, 0] = f0
-            spec[m, 1] = f1
-            factor[0] += f0[:half] * f0[:half] + f0[half:] * f0[half:]
-            factor[1] += f1[:half] * f1[:half] + f1[half:] * f1[half:]
-            return carry
-
-        lax.fori_loop(0, modes, forward, 0)
+            spec[p, m, 0] = f0
+            spec[p, m, 1] = f1
+            factor[p, 0] += f0[:half] * f0[:half] + f0[half:] * f0[half:]
+            factor[p, 1] += f1[:half] * f1[:half] + f1[half:] * f1[half:]
+        return carry
+
+    lax.fori_loop(0, modes, forward, 0, unroll=2)
+    for p in range(patterns):
         alive = live_ref[p].astype(jnp.float32)
-        factor[...] = (1.0 - root[p] / jnp.sqrt(factor[...] + smoothing)) * alive
-        placed[...] = jnp.zeros_like(placed)
-
-        def backward(out, first, j, carry):
-            group = first // keep
-            m = j ^ bit_ref[0] ^ bit_ref[1 + group]
-            scale0 = factor[0]
-            scale1 = factor[1]
-            e = left(spec[m, 0] * jnp.concatenate([scale0, scale0], axis=0), mats, 8)
-            o = left(spec[m, 1] * jnp.concatenate([scale1, scale1], axis=0), mats, 10)
+        factor[p] = (1.0 - root[p] / jnp.sqrt(factor[p] + smoothing)) * alive
+    placed[...] = jnp.zeros_like(placed)
+
+    def backward(out, first, j, carry):
+        group = first // keep
+        m = j ^ bit_ref[0] ^ bit_ref[1 + group]
+        q_re, q_im = probe[0, m], probe[1, m]
+        gains = [0.0, 0.0]
+        for p in range(patterns):
+            scale0, scale1 = factor[p, 0], factor[p, 1]
+            e = left(spec[p, m, 0] * jnp.concatenate([scale0, scale0], axis=0), mats, 8)
+            o = left(spec[p, m, 1] * jnp.concatenate([scale1, scale1], axis=0), mats, 10)
             total, other = e + o, e - o
             re = jnp.concatenate([total[:half], other[:half]], axis=0)
             im = jnp.concatenate([total[half:], other[half:]], axis=0)
@@ -144,28 +153,25 @@
             total, other = even + odd, even - odd
             x_re = jnp.concatenate([total[:, :half], other[:, :half]], axis=1)
             x_im = jnp.concatenate([total[:, half:], other[:, half:]], axis=1)
-            q_re, q_im = probe[0, m], probe[1, m]
-            placed[0, :width, :width] += q_re * x_re + q_im * x_im
-            placed[1, :width, :width] += q_re * x_im - q_im * x_re
-            o_re, o_im = patch[0], patch[1]
-            gains = (o_re * x_re + o_im * x_im, o_re * x_im - o_im * x_re)
-            for c in range(2):
-                for h in range(2):
-                    down = pl.multiple_of((h ^ bit_ref[5]) * half, half)
-                    at = (j - first, c ^ bit_ref[3 + group], pl.ds(down, half))
-                    value = gains[c][h * half : (h + 1) * half]
-                    if p == 0:
-                        out[at] = value
-                    else:
-                        out[at] = out[at] + value
-            return carry
-
-        quarter = modes // 4
-        for first, out in ((keep, send0), (0, keep0), (keep + quarter, send1), (quarter, keep1)):
-            lax.fori_loop(first, first + quarter, functools.partial(backward, out, first), 0)
+            placed[p, 0, :width, :width] += q_re * x_re + q_im * x_im
+            placed[p, 1, :width, :width] += q_re * x_im - q_im * x_re
+            o_re, o_im = patch[p, 0], patch[p, 1]
+            gains[0] += o_re * x_re + o_im * x_im
+            gains[1] += o_re * x_im - o_im * x_re
+        for c in range(2):
+            for h in range(2):
+                down = pl.multiple_of((h ^ bit_ref[5]) * half, half)
+                at = (j - first, c ^ bit_ref[3 + group], pl.ds(down, half))
+                out[at] = gains[c][h * half : (h + 1) * half]
+        return carry
+
+    quarter = modes // 4
+    for first, out in ((keep, send0), (0, keep0), (keep + quarter, send1), (quarter, keep1)):
+        lax.fori_loop(first, first + quarter, functools.partial(backward, out, first), 0, unroll=2)
+    for p, (top, drop, base, shift) in enumerate(corners):
         for c in range(2):
             at = (c, pl.ds(top, tall), pl.ds(base, wide))
-            grad[at] = grad[at] + pltpu.roll(pltpu.roll(placed[c], drop, 0), shift, 1)
+            grad[at] = grad[at] + pltpu.roll(pltpu.roll(placed[p, c], drop, 0), shift, 1)
 
     leaving = [
         pltpu.make_async_copy(src, dst, sems.at[i])
@@ -317,7 +323,7 @@
     bits = jnp.stack(
         [side * (modes // 2), kept_first * eighth, kept_second * eighth, kept_second, kept_first, bit_of(others[0])]
     ).astype(jnp.int32)
-    mats = jnp.asarray(matrices(width))
+    rights, lefts = matrices(width)
     g_own, g_beside, g_below, g_corner, keep0, keep1, send0, send1 = pl.pallas_call(
         kernel,
         out_shape=(
@@ -327,19 +333,19 @@
             jax.ShapeDtypeStruct((2, width, width), f32),
             *[jax.ShapeDtypeStruct((modes // 4, 2, width, width), f32)] * 4,
         ),
-        in_specs=[smem] * 4 + [hbm] * 5 + [vmem] * 3,
+        in_specs=[smem] * 4 + [hbm] * 5 + [vmem] * 4,
         out_specs=(*[hbm] * 4, *[vmem] * 4),
         scratch_shapes=[
             pltpu.VMEM((2, rows + width, cols + width), f32),
             pltpu.VMEM((2, rows + width, cols + width), f32),
-            pltpu.VMEM((modes, 2, width, width), f32),
-            pltpu.VMEM((2, width, width), f32),
-            pltpu.VMEM((2, half, width), f32),
-            pltpu.VMEM((2, width + 8, width + 128), f32),
+            pltpu.VMEM((patterns, modes, 2, width, width), f32),
+            pltpu.VMEM((patterns, 2, width, width), f32),
+            pltpu.VMEM((patterns, 2, half, width), f32),
+            pltpu.VMEM((patterns, 2, width + 8, width + 128), f32),
             pltpu.SemaphoreType.DMA((5,)),
         ],
         compiler_params=pltpu.CompilerParams(vmem_limit_bytes=48 * 1024 * 1024),
-    )(row_offset, col_offset, live, bits, object_field, beside, below0, below1, corner, probe, root, mats)
+    )(row_offset, col_offset, live, bits, object_field, beside, below0, below1, corner, probe, root, jnp.asarray(rights), jnp.asarray(lefts))
 
     below_grad = g_below.at[:, :, :width].add(passed_along(g_corner, "col", 1))
     from_left = passed_along(g_beside, "col", 1)

time: 151 us -> 144 us (0.954)
  Pallas kernels: 41.1 us -> 35.4 us
  local copies, waits for them, and re-layouts: 6.75 us -> 4.89 us
    pallas_call x1, Pallas kernels: 35.5 us -> 29.8 us  [shards(): pl.pallas_call(kernel, out_shape=(jax.ShapeDtypeStruct((2, rows, cols), f...]
  transfers between devices with their start and end apart: 27 -> 27, of which waited for: 13 -> 13; matrix products, arithmetic and copies ran while one was open for 4% -> 3% of each run, Pallas kernels for 2% -> 2%
where the time goes in v2:
time: 144 us
  waiting for transfers between devices  58.8 us (41%)
  starting transfers between devices  38.9 us (27%)
  Pallas kernels  35.4 us (25%)
  local copies, waits for them, and re-layouts  4.89 us (3%)
  between operations  3.26 us (2%)
  other arithmetic  2.46 us (2%)
    pallas_call x1, Pallas kernels, shards(): pl.pallas_call(kernel, out_shape=(jax.ShapeDtypeStruct((2, rows, cols), f...  29.8 us
    ppermute x8, waiting for transfers between devices, hop(): return lax.ppermute(array, ('row', 'col'), pairs)  26.4 us
    ppermute x7, waiting for transfers between devices, passed_along(): return lax.ppermute(array, axis, pairs)  25.7 us
    ppermute x12, starting transfers between devices, swap(): lax.ppermute(array, axis, [(i, i ^ 1 << bit) for i in range(lax.axis_size...  15.3 us
    ppermute x7, starting transfers between devices, passed_along(): return lax.ppermute(array, axis, pairs)  11.9 us
    ppermute x8, starting transfers between devices, hop(): return lax.ppermute(array, ('row', 'col'), pairs)  11.6 us
    ppermute x12, waiting for transfers between devices, swap(): lax.ppermute(array, axis, [(i, i ^ 1 << bit) for i in range(lax.axis_size...  6.73 us
  transfers between devices with their start and end apart: 27, of which 13 were waited for; matrix products, arithmetic and copies ran while one was open for 3% of the time, Pallas kernels for 2%

profile of v2, /device:TPU:0, one launch (start us, length us, event | category | flops | bytes accessed | tf_op | source)
XLA Modules:
  0.0 143.7 jit_solution(12129917284773256506)
XLA Ops:
  0.6 1.5 %fusion.8 = (f32[2,256,256]{2,1,0:T(8,128)S(1)}, f32[2,256,256]{2,1,0:T(8,128)S(1)}) fusion(f32[2,512,512]{2,1,0:T(8,128)} %own.1), kind=kLoop, calls=%fused_computation.29 | loop fusion | bytes 2097152 | tf_op jit(solution)/shard_map/slice | solution.py:305
  6.3 13.6 %collective-permute-done.1.below0 = f32[2,256,256]{2,1,0:T(8,128)S(1)} collective-permute-done((f32[2,256,256]{2,1,0:T(8,128)S(1)}, f32[2,256,256]{2,1,0:T(8,128)S(1)}, u32[]{:S(2)}, u32[]{:S(2)}) %collective-permute-start.1) | collective-permute-done | bytes 524320 | tf_op jit(solution)/shard_map/ppermute | solution.py:18
  21.2 2.8 %shard_map.104.root = f32[2,2,128,256]{3,2,1,0:T(8,128)} custom-call(f32[2,256,256]{2,1,0:T(8,128)} %intensity.1, bf16[2,256,256]{2,1,0:T(8,128)(2,1)} %constant.96.clone.orders), custom_call_target="tpu_custom_call" | custom-call | tf_op jit(solution)/shard_map/pallas_call | solution.py:313
  24.0 6.2 %collective-permute-done.2.below1 = f32[2,256,256]{2,1,0:T(8,128)S(1)} collective-permute-done((f32[2,256,256]{2,1,0:T(8,128)S(1)}, f32[2,256,256]{2,1,0:T(8,128)S(1)}, u32[]{:S(2)}, u32[]{:S(2)}) %collective-permute-start.2) | collective-permute-done | bytes 524320 | tf_op jit(solution)/shard_map/ppermute | solution.py:18
  31.3 29.8 %shard_map.105 = (f32[2,512,512]{2,1,0:T(8,128)}, f32[2,512,256]{2,1,0:T(8,128)S(1)}, f32[2,256,512]{2,1,0:T(8,128)S(1)}, f32[2,256,256]{2,1,0:T(8,128)S(1)}, f3...) custom-call(s32[2]{0:T(128)S(1)} %copy-done.1, ...), custom_call_target="tpu_custom_call" | custom-call | tf_op jit(solution)/shard_map/pallas_call | solution.py:327
  61.8 2.4 %collective-permute-done.6 = f32[2,2,256,256]{3,2,1,0:T(8,128)S(1)} collective-permute-done((f32[2,2,256,256]{3,2,1,0:T(8,128)}, f32[2,2,256,256]{3,2,1,0:T(8,128)S(1)}, u32[]{:S(2)}, u32[]{:S(2)}) %collective-permute-start.6) | collective-permute-done | bytes 1048608 | tf_op jit(solution)/shard_map/ppermute | solution.py:237
  64.3 2.5 %collective-permute-start.7 = (f32[1,2,256,256]{3,2,1,0:T(8,128)S(1)}, f32[1,2,256,256]{3,2,1,0:T(8,128)S(1)}, u32[]{:S(2)}, u32[]{:S(2)}) collective-permute-start(f32[1,2,256,256]{3,2,1,0:T(8,128)S(1)} %slice_add_fusion.2), channel_id=1, source_target_pairs={{0,8},{1,17},{2,10},{3,19},{4,12},{5,21},{6,14},{7,23},{8,0},{9,25... | collective-permute-start | bytes 1572872 | tf_op jit(solution)/shard_map/ppermute | solution.py:255
  70.7 3.3 %collective-permute-done.7 = f32[1,2,256,256]{3,2,1,0:T(8,128)S(1)} collective-permute-done((f32[1,2,256,256]{3,2,1,0:T(8,128)S(1)}, f32[1,2,256,256]{3,2,1,0:T(8,128)S(1)}, u32[]{:S(2)}, u32[]{:S(2)}) %collective-permute-start.7) | collective-permute-done | bytes 524320 | tf_op jit(solution)/shard_map/ppermute | solution.py:255
  75.2 7.2 %collective-permute-done.10 = f32[1,2,256,256]{3,2,1,0:T(8,128)S(1)} collective-permute-done((f32[1,2,256,256]{3,2,1,0:T(8,128)S(1)}, f32[1,2,256,256]{3,2,1,0:T(8,128)S(1)}, u32[]{:S(2)}, u32[]{:S(2)}) %collective-permute-start.10) | collective-permute-done | bytes 524320 | tf_op jit(solution)/shard_map/ppermute | solution.py:255
  84.6 1.6 %collective-permute-start.13 = (f32[1,128,256]{2,1,0:T(8,128)S(1)}, f32[1,128,256]{2,1,0:T(8,128)S(1)}, u32[]{:S(2)}, u32[]{:S(2)}) collective-permute-start(f32[1,128,256]{2,1,0:T(8,128)S(1)} %slice.191), channel_id=1, source_target_pairs={{0,2},{1,3},{2,0},{3,1},{4,6},{5,7},{6,4},{7,5},{8,10},{9,11},{10,... | collective-permute-start | bytes 393224 | tf_op jit(solution)/shard_map/ppermute | solution.py:237
  86.3 2.6 %collective-permute-done.11 = f32[1,256,256]{2,1,0:T(8,128)S(1)} collective-permute-done((f32[1,256,256]{2,1,0:T(8,128)S(1)}, f32[1,256,256]{2,1,0:T(8,128)S(1)}, u32[]{:S(2)}, u32[]{:S(2)}) %collective-permute-start.11) | collective-permute-done | bytes 262176 | tf_op jit(solution)/shard_map/ppermute | solution.py:255
  91.0 4.0 %collective-permute-start.12 = (f32[2,256,512]{2,1,0:T(8,128)S(1)}, f32[2,256,512]{2,1,0:T(8,128)S(1)}, u32[]{:S(2)}, u32[]{:S(2)}) collective-permute-start(f32[2,256,512]{2,1,0:T(8,128)S(1)} %add_add_fusion), channel_id=1, source_target_pairs={{0,8},{8,16},{16,24},{1,9},{9,17},{17,25},{2,10},{10,18},{18,26},{... | collective-permute-start | bytes 3145736 | tf_op jit(solution)/shard_map/ppermute | solution.py:18
  95.1 1.6 %collective-permute-start.18 = (f32[1,128,256]{2,1,0:T(8,128)S(1)}, f32[1,128,256]{2,1,0:T(8,128)S(1)}, u32[]{:S(2)}, u32[]{:S(2)}) collective-permute-start(f32[1,128,256]{2,1,0:T(8,128)S(1)} %slice.195), channel_id=1, source_target_pairs={{0,2},{1,3},{2,0},{3,1},{4,6},{5,7},{6,4},{7,5},{8,10},{9,11},{10,... | collective-permute-start | bytes 393224 | tf_op jit(solution)/shard_map/ppermute | solution.py:237
  96.8 2.6 %collective-permute-start.14 = (f32[1,128,256]{2,1,0:T(8,128)S(1)}, f32[1,128,256]{2,1,0:T(8,128)S(1)}, u32[]{:S(2)}, u32[]{:S(2)}) collective-permute-start(f32[1,128,256]{2,1,0:T(8,128)S(1)} %slice_add_fusion.12), channel_id=1, source_target_pairs={{0,4},{1,5},{2,6},{3,7},{4,0},{5,1},{6,2},{7,3},{8,12},{9,13},{10,... | collective-permute-start | bytes 393224 | tf_op jit(solution)/shard_map/ppermute | solution.py:237
  99.4 1.8 %collective-permute-done.18 = f32[1,128,256]{2,1,0:T(8,128)S(1)} collective-permute-done((f32[1,128,256]{2,1,0:T(8,128)S(1)}, f32[1,128,256]{2,1,0:T(8,128)S(1)}, u32[]{:S(2)}, u32[]{:S(2)}) %collective-permute-start.18) | collective-permute-done | bytes 131104 | tf_op jit(solution)/shard_map/ppermute | solution.py:237
  101.2 2.4 %collective-permute-start.19 = (f32[1,128,256]{2,1,0:T(8,128)S(1)}, f32[1,128,256]{2,1,0:T(8,128)S(1)}, u32[]{:S(2)}, u32[]{:S(2)}) collective-permute-start(f32[1,128,256]{2,1,0:T(8,128)S(1)} %slice_add_fusion.11), channel_id=1, source_target_pairs={{0,4},{1,5},{2,6},{3,7},{4,0},{5,1},{6,2},{7,3},{8,12},{9,13},{10,... | collective-permute-start | bytes 393224 | tf_op jit(solution)/shard_map/ppermute | solution.py:237
  104.1 2.3 %collective-permute-start.15 = (f32[1,128,256]{2,1,0:T(8,128)S(1)}, f32[1,128,256]{2,1,0:T(8,128)S(1)}, u32[]{:S(2)}, u32[]{:S(2)}) collective-permute-start(f32[1,128,256]{2,1,0:T(8,128)S(1)} %add.206), channel_id=1, source_target_pairs={{0,2},{1,3},{2,0},{3,1},{4,6},{5,7},{6,4},{7,5},{8,10},{9,11},{10,... | collective-permute-start | bytes 393224 | tf_op jit(solution)/shard_map/ppermute | solution.py:237
  107.3 3.4 %collective-permute-start.20 = (f32[1,128,256]{2,1,0:T(8,128)S(1)}, f32[1,128,256]{2,1,0:T(8,128)S(1)}, u32[]{:S(2)}, u32[]{:S(2)}) collective-permute-start(f32[1,128,256]{2,1,0:T(8,128)S(1)} %add.212), channel_id=1, source_target_pairs={{0,2},{1,3},{2,0},{3,1},{4,6},{5,7},{6,4},{7,5},{8,10},{9,11},{10,... | collective-permute-start | bytes 393224 | tf_op jit(solution)/shard_map/ppermute | solution.py:237
  112.2 5.9 %collective-permute-done.12 = f32[2,256,512]{2,1,0:T(8,128)S(1)} collective-permute-done((f32[2,256,512]{2,1,0:T(8,128)S(1)}, f32[2,256,512]{2,1,0:T(8,128)S(1)}, u32[]{:S(2)}, u32[]{:S(2)}) %collective-permute-start.12) | collective-permute-done | bytes 1048608 | tf_op jit(solution)/shard_map/ppermute | solution.py:18
  119.7 1.7 %collective-permute-start.21 = (f32[1,256,256]{2,1,0:T(8,128)S(1)}, f32[1,256,256]{2,1,0:T(8,128)S(1)}, u32[]{:S(2)}, u32[]{:S(2)}) collective-permute-start(f32[1,256,256]{2,1,0:T(8,128)S(1)} %maximum_add_fusion.1), channel_id=1, source_target_pairs={{0,16},{1,9},{2,18},{3,11},{4,20},{5,13},{6,22},{7,15},{8,24},{9,1... | collective-permute-start | bytes 786440 | tf_op jit(solution)/shard_map/ppermute | solution.py:255
  122.4 6.6 %collective-permute-done.21 = f32[1,256,256]{2,1,0:T(8,128)S(1)} collective-permute-done((f32[1,256,256]{2,1,0:T(8,128)S(1)}, f32[1,256,256]{2,1,0:T(8,128)S(1)}, u32[]{:S(2)}, u32[]{:S(2)}) %collective-permute-start.21) | collective-permute-done | bytes 262176 | tf_op jit(solution)/shard_map/ppermute | solution.py:255
  129.1 2.5 %collective-permute-start.22 = (f32[1,2,256,256]{3,2,1,0:T(8,128)S(1)}, f32[1,2,256,256]{3,2,1,0:T(8,128)S(1)}, u32[]{:S(2)}, u32[]{:S(2)}) collective-permute-start(f32[1,2,256,256]{3,2,1,0:T(8,128)S(1)} %pad_maximum_fusion.1.refs_2_), channel_id=1, source_target_pairs={{0,8},{1,17},{2,10},{3,19},{4,12},{5,21},{6,14},{7,23},{8,0},{9,25... | collective-permute-start | bytes 1572872 | tf_op jit(solution)/shard_map/ppermute | solution.py:255
  132.1 6.6 %collective-permute-done.22.refs_3_ = f32[1,2,256,256]{3,2,1,0:T(8,128)S(1)} collective-permute-done((f32[1,2,256,256]{3,2,1,0:T(8,128)S(1)}, f32[1,2,256,256]{3,2,1,0:T(8,128)S(1)}, u32[]{:S(2)}, u32[]{:S(2)}) %collective-permute-start.22) | collective-permute-done | bytes 524320 | tf_op jit(solution)/shard_map/ppermute | solution.py:255
  140.7 2.8 %shard_map.106 = f32[2,8,256,256]{3,2,1,0:T(8,128)} custom-call(s32[6]{0:T(128)S(1)} %stack.37.bit_ref, f32[1,2,256,256]{3,2,1,0:T(8,128)S(1)} %pad_maximum_fusion.refs_0_, f32[1,2,256,256]{3,2,1,0:T(8,128)S(1)} %collective-permute-done.17.refs_1_, f32[1,2,256,256]{3,2,1,0:T(8,128)S(1)} %pad_maximum_fusion.1.refs_2_, ...), custom_call_target="tpu_custom_call" | custom-call | tf_op jit(solution)/shard_map/pallas_call | solution.py:282
  (79 shorter events, 22.5 us)
Async XLA Ops:
  2.1 17.7 %collective-permute-start.1 = (f32[2,256,256]{2,1,0:T(8,128)S(1)}, f32[2,256,256]{2,1,0:T(8,128)S(1)}, u32[]{:S(2)}, u32[]{:S(2)}) collective-permute-start(f32[2,256,256]{2,1,0:T(8,128)S(1)} %get-tuple-element.55), channel_id=1, source_target_pairs={{8,0},{16,8},{24,16},{9,1},{17,9},{25,17},{10,2},{18,10},{26,18},{... | collective-permute-start | bytes 1572872 | tf_op jit(solution)/shard_map/ppermute | solution.py:18
  3.7 26.6 %collective-permute-start = (f32[2,512,256]{2,1,0:T(8,128)S(1)}, f32[2,512,256]{2,1,0:T(8,128)}, u32[]{:S(2)}, u32[]{:S(2)}) collective-permute-start(f32[2,512,256]{2,1,0:T(8,128)S(1)} %slice.150), channel_id=1, source_target_pairs={{1,0},{2,1},{3,2},{4,3},{5,4},{6,5},{7,6},{9,8},{10,9},{11,10},{12... | collective-permute-start | bytes 3145736 | tf_op jit(solution)/shard_map/ppermute | solution.py:18
  5.0 25.3 %collective-permute-start.2 = (f32[2,256,256]{2,1,0:T(8,128)S(1)}, f32[2,256,256]{2,1,0:T(8,128)S(1)}, u32[]{:S(2)}, u32[]{:S(2)}) collective-permute-start(f32[2,256,256]{2,1,0:T(8,128)S(1)} %get-tuple-element.54), channel_id=1, source_target_pairs={{8,0},{16,8},{24,16},{9,1},{17,9},{25,17},{10,2},{18,10},{26,18},{... | collective-permute-start | bytes 1572872 | tf_op jit(solution)/shard_map/ppermute | solution.py:18
  19.9 10.4 %collective-permute-start.3 = (f32[2,256,256]{2,1,0:T(8,128)S(1)}, f32[2,256,256]{2,1,0:T(8,128)S(1)}, u32[]{:S(2)}, u32[]{:S(2)}) collective-permute-start(f32[2,256,256]{2,1,0:T(8,128)S(1)} %collective-permute-done.1.below0), channel_id=1, source_target_pairs={{1,0},{2,1},{3,2},{4,3},{5,4},{6,5},{7,6},{9,8},{10,9},{11,10},{12... | collective-permute-start | bytes 1572872 | tf_op jit(solution)/shard_map/ppermute | solution.py:18
  64.3 9.7 %collective-permute-start.7 = (f32[1,2,256,256]{3,2,1,0:T(8,128)S(1)}, f32[1,2,256,256]{3,2,1,0:T(8,128)S(1)}, u32[]{:S(2)}, u32[]{:S(2)}) collective-permute-start(f32[1,2,256,256]{3,2,1,0:T(8,128)S(1)} %slice_add_fusion.2), channel_id=1, source_target_pairs={{0,8},{1,17},{2,10},{3,19},{4,12},{5,21},{6,14},{7,23},{8,0},{9,25... | collective-permute-start | bytes 1572872 | tf_op jit(solution)/shard_map/ppermute | solution.py:255
  67.9 14.5 %collective-permute-start.10 = (f32[1,2,256,256]{3,2,1,0:T(8,128)S(1)}, f32[1,2,256,256]{3,2,1,0:T(8,128)S(1)}, u32[]{:S(2)}, u32[]{:S(2)}) collective-permute-start(f32[1,2,256,256]{3,2,1,0:T(8,128)S(1)} %slice_add_fusion.1), channel_id=1, source_target_pairs={{0,8},{1,17},{2,10},{3,19},{4,12},{5,21},{6,14},{7,23},{8,0},{9,25... | collective-permute-start | bytes 1572872 | tf_op jit(solution)/shard_map/ppermute | solution.py:255
  69.4 14.3 %collective-permute-start.5 = (f32[2,256,256]{2,1,0:T(8,128)S(1)}, f32[2,256,256]{2,1,0:T(8,128)S(1)}, u32[]{:S(2)}, u32[]{:S(2)}) collective-permute-start(f32[2,256,256]{2,1,0:T(8,128)S(1)} %get-tuple-element.49), channel_id=1, source_target_pairs={{0,1},{1,2},{2,3},{3,4},{4,5},{5,6},{6,7},{8,9},{9,10},{10,11},{11... | collective-permute-start | bytes 1572872 | tf_op jit(solution)/shard_map/ppermute | solution.py:18
  74.0 9.8 %collective-permute-start.8 = (f32[1,256,256]{2,1,0:T(8,128)S(1)}, f32[1,256,256]{2,1,0:T(8,128)S(1)}, u32[]{:S(2)}, u32[]{:S(2)}) collective-permute-start(f32[1,256,256]{2,1,0:T(8,128)S(1)} %fusion.6), channel_id=1, source_target_pairs={{0,16},{1,9},{2,18},{3,11},{4,20},{5,13},{6,22},{7,15},{8,24},{9,1... | collective-permute-start | bytes 786440 | tf_op jit(solution)/shard_map/ppermute | solution.py:255
  82.5 6.4 %collective-permute-start.11 = (f32[1,256,256]{2,1,0:T(8,128)S(1)}, f32[1,256,256]{2,1,0:T(8,128)S(1)}, u32[]{:S(2)}, u32[]{:S(2)}) collective-permute-start(f32[1,256,256]{2,1,0:T(8,128)S(1)} %fusion.5), channel_id=1, source_target_pairs={{0,16},{1,9},{2,18},{3,11},{4,20},{5,13},{6,22},{7,15},{8,24},{9,1... | collective-permute-start | bytes 786440 | tf_op jit(solution)/shard_map/ppermute | solution.py:255
  84.6 12.1 %collective-permute-start.13 = (f32[1,128,256]{2,1,0:T(8,128)S(1)}, f32[1,128,256]{2,1,0:T(8,128)S(1)}, u32[]{:S(2)}, u32[]{:S(2)}) collective-permute-start(f32[1,128,256]{2,1,0:T(8,128)S(1)} %slice.191), channel_id=1, source_target_pairs={{0,2},{1,3},{2,0},{3,1},{4,6},{5,7},{6,4},{7,5},{8,10},{9,11},{10,... | collective-permute-start | bytes 393224 | tf_op jit(solution)/shard_map/ppermute | solution.py:237
  91.0 27.1 %collective-permute-start.12 = (f32[2,256,512]{2,1,0:T(8,128)S(1)}, f32[2,256,512]{2,1,0:T(8,128)S(1)}, u32[]{:S(2)}, u32[]{:S(2)}) collective-permute-start(f32[2,256,512]{2,1,0:T(8,128)S(1)} %add_add_fusion), channel_id=1, source_target_pairs={{0,8},{8,16},{16,24},{1,9},{9,17},{17,25},{2,10},{10,18},{18,26},{... | collective-permute-start | bytes 3145736 | tf_op jit(solution)/shard_map/ppermute | solution.py:18
  95.1 6.1 %collective-permute-start.18 = (f32[1,128,256]{2,1,0:T(8,128)S(1)}, f32[1,128,256]{2,1,0:T(8,128)S(1)}, u32[]{:S(2)}, u32[]{:S(2)}) collective-permute-start(f32[1,128,256]{2,1,0:T(8,128)S(1)} %slice.195), channel_id=1, source_target_pairs={{0,2},{1,3},{2,0},{3,1},{4,6},{5,7},{6,4},{7,5},{8,10},{9,11},{10,... | collective-permute-start | bytes 393224 | tf_op jit(solution)/shard_map/ppermute | solution.py:237
  96.8 7.3 %collective-permute-start.14 = (f32[1,128,256]{2,1,0:T(8,128)S(1)}, f32[1,128,256]{2,1,0:T(8,128)S(1)}, u32[]{:S(2)}, u32[]{:S(2)}) collective-permute-start(f32[1,128,256]{2,1,0:T(8,128)S(1)} %slice_add_fusion.12), channel_id=1, source_target_pairs={{0,4},{1,5},{2,6},{3,7},{4,0},{5,1},{6,2},{7,3},{8,12},{9,13},{10,... | collective-permute-start | bytes 393224 | tf_op jit(solution)/shard_map/ppermute | solution.py:237
  101.2 6.0 %collective-permute-start.19 = (f32[1,128,256]{2,1,0:T(8,128)S(1)}, f32[1,128,256]{2,1,0:T(8,128)S(1)}, u32[]{:S(2)}, u32[]{:S(2)}) collective-permute-start(f32[1,128,256]{2,1,0:T(8,128)S(1)} %slice_add_fusion.11), channel_id=1, source_target_pairs={{0,4},{1,5},{2,6},{3,7},{4,0},{5,1},{6,2},{7,3},{8,12},{9,13},{10,... | collective-permute-start | bytes 393224 | tf_op jit(solution)/shard_map/ppermute | solution.py:237
  104.1 6.6 %collective-permute-start.15 = (f32[1,128,256]{2,1,0:T(8,128)S(1)}, f32[1,128,256]{2,1,0:T(8,128)S(1)}, u32[]{:S(2)}, u32[]{:S(2)}) collective-permute-start(f32[1,128,256]{2,1,0:T(8,128)S(1)} %add.206), channel_id=1, source_target_pairs={{0,2},{1,3},{2,0},{3,1},{4,6},{5,7},{6,4},{7,5},{8,10},{9,11},{10,... | collective-permute-start | bytes 393224 | tf_op jit(solution)/shard_map/ppermute | solution.py:237
  107.3 12.4 %collective-permute-start.20 = (f32[1,128,256]{2,1,0:T(8,128)S(1)}, f32[1,128,256]{2,1,0:T(8,128)S(1)}, u32[]{:S(2)}, u32[]{:S(2)}) collective-permute-start(f32[1,128,256]{2,1,0:T(8,128)S(1)} %add.212), channel_id=1, source_target_pairs={{0,2},{1,3},{2,0},{3,1},{4,6},{5,7},{6,4},{7,5},{8,10},{9,11},{10,... | collective-permute-start | bytes 393224 | tf_op jit(solution)/shard_map/ppermute | solution.py:237
  110.7 10.7 %collective-permute-start.16 = (f32[1,256,256]{2,1,0:T(8,128)S(1)}, f32[1,256,256]{2,1,0:T(8,128)S(1)}, u32[]{:S(2)}, u32[]{:S(2)}) collective-permute-start(f32[1,256,256]{2,1,0:T(8,128)S(1)} %get-tuple-element.57), channel_id=1, source_target_pairs={{0,16},{1,9},{2,18},{3,11},{4,20},{5,13},{6,22},{7,15},{8,24},{9,1... | collective-permute-start | bytes 786440 | tf_op jit(solution)/shard_map/ppermute | solution.py:255
  110.8 28.0 %collective-permute-start.4 = (f32[2,512,256]{2,1,0:T(8,128)S(1)}, f32[2,512,256]{2,1,0:T(8,128)S(1)}, u32[]{:S(2)}, u32[]{:S(2)}) collective-permute-start(f32[2,512,256]{2,1,0:T(8,128)S(1)} %get-tuple-element.47), channel_id=1, source_target_pairs={{0,1},{1,2},{2,3},{3,4},{4,5},{5,6},{6,7},{8,9},{9,10},{10,11},{11... | collective-permute-start | bytes 3145736 | tf_op jit(solution)/shard_map/ppermute | solution.py:18
  119.7 9.3 %collective-permute-start.21 = (f32[1,256,256]{2,1,0:T(8,128)S(1)}, f32[1,256,256]{2,1,0:T(8,128)S(1)}, u32[]{:S(2)}, u32[]{:S(2)}) collective-permute-start(f32[1,256,256]{2,1,0:T(8,128)S(1)} %maximum_add_fusion.1), channel_id=1, source_target_pairs={{0,16},{1,9},{2,18},{3,11},{4,20},{5,13},{6,22},{7,15},{8,24},{9,1... | collective-permute-start | bytes 786440 | tf_op jit(solution)/shard_map/ppermute | solution.py:255
  121.5 10.1 %collective-permute-start.17 = (f32[1,2,256,256]{3,2,1,0:T(8,128)S(1)}, f32[1,2,256,256]{3,2,1,0:T(8,128)S(1)}, u32[]{:S(2)}, u32[]{:S(2)}) collective-permute-start(f32[1,2,256,256]{3,2,1,0:T(8,128)S(1)} %pad_maximum_fusion.refs_0_), channel_id=1, source_target_pairs={{0,8},{1,17},{2,10},{3,19},{4,12},{5,21},{6,14},{7,23},{8,0},{9,25... | collective-permute-start | bytes 1572872 | tf_op jit(solution)/shard_map/ppermute | solution.py:255
  129.1 9.7 %collective-permute-start.22 = (f32[1,2,256,256]{3,2,1,0:T(8,128)S(1)}, f32[1,2,256,256]{3,2,1,0:T(8,128)S(1)}, u32[]{:S(2)}, u32[]{:S(2)}) collective-permute-start(f32[1,2,256,256]{3,2,1,0:T(8,128)S(1)} %pad_maximum_fusion.1.refs_2_), channel_id=1, source_target_pairs={{0,8},{1,17},{2,10},{3,19},{4,12},{5,21},{6,14},{7,23},{8,0},{9,25... | collective-permute-start | bytes 1572872 | tf_op jit(solution)/shard_map/ppermute | solution.py:255
  131.6 7.8 %collective-permute-start.23 = (f32[1,2,256,256]{3,2,1,0:T(8,128)S(1)}, f32[1,2,256,256]{3,2,1,0:T(8,128)S(1)}, u32[]{:S(2)}, u32[]{:S(2)}) collective-permute-start(f32[1,2,256,256]{3,2,1,0:T(8,128)S(1)} %pad_maximum_fusion.refs_0_), channel_id=1, source_target_pairs={{0,1},{1,0},{2,3},{3,2},{4,5},{5,4},{6,7},{7,6},{8,9},{9,8},{10,11... | collective-permute-start | bytes 1572872 | tf_op jit(solution)/shard_map/ppermute | solution.py:237
  131.6 7.8 %collective-permute-start.24 = (f32[1,2,256,256]{3,2,1,0:T(8,128)S(1)}, f32[1,2,256,256]{3,2,1,0:T(8,128)S(1)}, u32[]{:S(2)}, u32[]{:S(2)}) collective-permute-start(f32[1,2,256,256]{3,2,1,0:T(8,128)S(1)} %collective-permute-done.17.refs_1_), channel_id=1, source_target_pairs={{0,1},{1,0},{2,3},{3,2},{4,5},{5,4},{6,7},{7,6},{8,9},{9,8},{10,11... | collective-permute-start | bytes 1572872 | tf_op jit(solution)/shard_map/ppermute | solution.py:237
  132.1 7.3 %collective-permute-start.25 = (f32[1,2,256,256]{3,2,1,0:T(8,128)S(1)}, f32[1,2,256,256]{3,2,1,0:T(8,128)S(1)}, u32[]{:S(2)}, u32[]{:S(2)}) collective-permute-start(f32[1,2,256,256]{3,2,1,0:T(8,128)S(1)} %pad_maximum_fusion.1.refs_2_), channel_id=1, source_target_pairs={{0,1},{1,0},{2,3},{3,2},{4,5},{5,4},{6,7},{7,6},{8,9},{9,8},{10,11... | collective-permute-start | bytes 1572872 | tf_op jit(solution)/shard_map/ppermute | solution.py:237
  (11 other events, 141.3 us)

commit v3 on v2

--- a/solution.py
+++ b/solution.py
@@ -61,9 +61,9 @@
 
 
 def kernel(
-    row_ref, col_ref, live_ref, bit_ref, own, beside, below0, below1, corner, probe, root, rights, lefts,
+    row_ref, col_ref, live_ref, bit_ref, own, beside, below0, below1, corner, probe_in, root_in, rights, lefts,
     g_own, g_beside, g_below, g_corner, keep0, keep1, send0, send1,
-    ext, grad, spec, patch, factor, placed, sems,
+    ext, grad, spec, patch, factor, placed, probe, root, sems, probe_sems,
 ):
     mats = (rights, lefts)
     patterns, width = root.shape[0], root.shape[-1]
@@ -89,6 +89,14 @@
     ]
     for copy in arriving:
         copy.start()
+
+    def mode_copy(m):
+        return pltpu.make_async_copy(probe_in.at[:, m], probe.at[:, m], probe_sems.at[m])
+
+    for m in range(modes):
+        mode_copy(m).start()
+    root_copy = pltpu.make_async_copy(root_in, root, sems.at[5])
+    root_copy.start()
     grad[...] = jnp.zeros_like(grad)
     for copy in arriving:
         copy.wait()
@@ -111,6 +119,7 @@
     factor[...] = jnp.zeros_like(factor)
 
     def forward(m, carry):
+        mode_copy(m).wait()
         q_re, q_im = probe[0, m], probe[1, m]
         for p in range(patterns):
             o_re, o_im = patch[p, 0], patch[p, 1]
@@ -131,6 +140,7 @@
         return carry
 
     lax.fori_loop(0, modes, forward, 0, unroll=2)
+    root_copy.wait()
     for p in range(patterns):
         alive = live_ref[p].astype(jnp.float32)
         factor[p] = (1.0 - root[p] / jnp.sqrt(factor[p] + smoothing)) * alive
@@ -255,7 +265,7 @@
     return lax.ppermute(array, ("row", "col"), pairs)
 
 
-def probe_sum(kept, sent, bits, core, third, rest, below_grad):
+def probe_sum(kept, sent, bits, core, third, rest, below_grad, from_left):
     one = kept[0].shape[0] // 2
     half = kept[0].shape[-1] // 2
     totals = []
@@ -267,6 +277,7 @@
         totals.append(keep[:one, 0] + came[:one, 0] + came1[:, 0] + came2)
     from_above = passed_along(below_grad, "row", 1)
     own = []
+    totals[0] = after(totals[0], from_left)
     for number, total in enumerate(totals):
         total = total[:, :half] + swap(total[:, half:], third)
         for where in rest:
@@ -333,7 +344,7 @@
             jax.ShapeDtypeStruct((2, width, width), f32),
             *[jax.ShapeDtypeStruct((modes // 4, 2, width, width), f32)] * 4,
         ),
-        in_specs=[smem] * 4 + [hbm] * 5 + [vmem] * 4,
+        in_specs=[smem] * 4 + [hbm] * 7 + [vmem] * 2,
         out_specs=(*[hbm] * 4, *[vmem] * 4),
         scratch_shapes=[
             pltpu.VMEM((2, rows + width, cols + width), f32),
@@ -342,7 +353,10 @@
             pltpu.VMEM((patterns, 2, width, width), f32),
             pltpu.VMEM((patterns, 2, half, width), f32),
             pltpu.VMEM((patterns, 2, width + 8, width + 128), f32),
-            pltpu.SemaphoreType.DMA((5,)),
+            pltpu.VMEM(probe.shape, f32),
+            pltpu.VMEM((patterns, 2, half, width), f32),
+            pltpu.SemaphoreType.DMA((6,)),
+            pltpu.SemaphoreType.DMA((modes,)),
         ],
         compiler_params=pltpu.CompilerParams(vmem_limit_bytes=48 * 1024 * 1024),
     )(row_offset, col_offset, live, bits, object_field, beside, below0, below1, corner, probe, root, jnp.asarray(rights), jnp.asarray(lefts))
@@ -350,7 +364,7 @@
     below_grad = g_below.at[:, :, :width].add(passed_along(g_corner, "col", 1))
     from_left = passed_along(g_beside, "col", 1)
     probe_grad, from_above = probe_sum(
-        (keep0, keep1), (send0, send1), bits, core, others[0], others[1:], below_grad
+        (keep0, keep1), (send0, send1), bits, core, others[0], others[1:], below_grad, from_left
     )
     object_grad = g_own.at[:, :, :width].add(from_left)
     object_grad = object_grad.at[:, :width, :].add(from_above)

time: 144 us -> 144 us (level)
  starting transfers between devices: 38.9 us -> 36.7 us
    ppermute x12, starting transfers between devices: 15.3 us -> 9.79 us  [swap(): lax.ppermute(array, axis, [(i, i ^ 1 << bit) for i in range(lax.axis_size...]
    ppermute x12, waiting for transfers between devices: 6.73 us -> 12.3 us  [swap(): lax.ppermute(array, axis, [(i, i ^ 1 << bit) for i in range(lax.axis_size...]
    ppermute x8, waiting for transfers between devices: 26.4 us -> 23.3 us  [hop(): return lax.ppermute(array, ('row', 'col'), pairs)]
    ppermute x7, waiting for transfers between devices: 25.7 us -> 23.6 us  [passed_along(): return lax.ppermute(array, axis, pairs)]
    ppermute x8, starting transfers between devices: 11.6 us -> 13.3 us  [hop(): return lax.ppermute(array, ('row', 'col'), pairs)]
    ppermute x7, starting transfers between devices: 11.9 us -> 13.6 us  [passed_along(): return lax.ppermute(array, axis, pairs)]
  transfers between devices with their start and end apart: 27 -> 27, of which waited for: 13 -> 12; matrix products, arithmetic and copies ran while one was open for 3% -> 4% of each run, Pallas kernels for 2% -> 2%
where the time goes in v3:
time: 144 us; the launch traced here: 143 us
  waiting for transfers between devices  59.2 us (41%)
  starting transfers between devices  36.7 us (25%)
  Pallas kernels  34.9 us (24%)
  local copies, waits for them, and re-layouts  5.88 us (4%)
  between operations  3.93 us (3%)
  other arithmetic  2.45 us (2%)
    pallas_call x1, Pallas kernels, shards(): pl.pallas_call(kernel, out_shape=(jax.ShapeDtypeStruct((2, rows, cols), f...  29.3 us
    ppermute x7, waiting for transfers between devices, passed_along(): return lax.ppermute(array, axis, pairs)  23.6 us
    ppermute x8, waiting for transfers between devices, hop(): return lax.ppermute(array, ('row', 'col'), pairs)  23.3 us
    ppermute x7, starting transfers between devices, passed_along(): return lax.ppermute(array, axis, pairs)  13.6 us
    ppermute x8, starting transfers between devices, hop(): return lax.ppermute(array, ('row', 'col'), pairs)  13.3 us
    ppermute x12, waiting for transfers between devices, swap(): lax.ppermute(array, axis, [(i, i ^ 1 << bit) for i in range(lax.axis_size...  12.3 us
    ppermute x12, starting transfers between devices, swap(): lax.ppermute(array, axis, [(i, i ^ 1 << bit) for i in range(lax.axis_size...  9.79 us
  transfers between devices with their start and end apart: 27, of which 12 were waited for; matrix products, arithmetic and copies ran while one was open for 4% of the time, Pallas kernels for 2%

profile of v3, /device:TPU:0, one launch (start us, length us, event | category | flops | bytes accessed | tf_op | source)
XLA Modules:
  0.0 143.1 jit_solution(698983794056739594)
XLA Ops:
  6.3 13.6 %collective-permute-done.1.below0 = f32[2,256,256]{2,1,0:T(8,128)S(1)} collective-permute-done((f32[2,256,256]{2,1,0:T(8,128)S(1)}, f32[2,256,256]{2,1,0:T(8,128)S(1)}, u32[]{:S(2)}, u32[]{:S(2)}) %collective-permute-start.1) | collective-permute-done | bytes 524320 | tf_op jit(solution)/shard_map/ppermute | solution.py:18
  21.2 2.8 %shard_map.104.root_in = f32[2,2,128,256]{3,2,1,0:T(8,128)} custom-call(f32[2,256,256]{2,1,0:T(8,128)} %intensity.1, bf16[2,256,256]{2,1,0:T(8,128)(2,1)} %constant.97.clone.orders), custom_call_target="tpu_custom_call" | custom-call | tf_op jit(solution)/shard_map/pallas_call | solution.py:324
  24.0 6.2 %collective-permute-done.2.below1 = f32[2,256,256]{2,1,0:T(8,128)S(1)} collective-permute-done((f32[2,256,256]{2,1,0:T(8,128)S(1)}, f32[2,256,256]{2,1,0:T(8,128)S(1)}, u32[]{:S(2)}, u32[]{:S(2)}) %collective-permute-start.2) | collective-permute-done | bytes 524320 | tf_op jit(solution)/shard_map/ppermute | solution.py:18
  31.3 29.3 %shard_map.105 = (f32[2,512,512]{2,1,0:T(8,128)}, f32[2,512,256]{2,1,0:T(8,128)S(1)}, f32[2,256,512]{2,1,0:T(8,128)S(1)}, f32[2,256,256]{2,1,0:T(8,128)S(1)}, f3...) custom-call(s32[2]{0:T(128)S(1)} %copy-done.1, ...), custom_call_target="tpu_custom_call" | custom-call | tf_op jit(solution)/shard_map/pallas_call | solution.py:338
  61.4 2.4 %collective-permute-start.4 = (f32[2,512,256]{2,1,0:T(8,128)S(1)}, f32[2,512,256]{2,1,0:T(8,128)S(1)}, u32[]{:S(2)}, u32[]{:S(2)}) collective-permute-start(f32[2,512,256]{2,1,0:T(8,128)S(1)} %get-tuple-element.47), channel_id=1, source_target_pairs={{0,1},{1,2},{2,3},{3,4},{4,5},{5,6},{6,7},{8,9},{9,10},{10,11},{11... | collective-permute-start | bytes 3145736 | tf_op jit(solution)/shard_map/ppermute | solution.py:18
  63.9 2.5 %collective-permute-start.7 = (f32[1,2,256,256]{3,2,1,0:T(8,128)S(1)}, f32[1,2,256,256]{3,2,1,0:T(8,128)S(1)}, u32[]{:S(2)}, u32[]{:S(2)}) collective-permute-start(f32[1,2,256,256]{3,2,1,0:T(8,128)S(1)} %slice_add_fusion.2), channel_id=1, source_target_pairs={{0,8},{1,17},{2,10},{3,19},{4,12},{5,21},{6,14},{7,23},{8,0},{9,25... | collective-permute-start | bytes 1572872 | tf_op jit(solution)/shard_map/ppermute | solution.py:265
  70.2 3.3 %collective-permute-done.7 = f32[1,2,256,256]{3,2,1,0:T(8,128)S(1)} collective-permute-done((f32[1,2,256,256]{3,2,1,0:T(8,128)S(1)}, f32[1,2,256,256]{3,2,1,0:T(8,128)S(1)}, u32[]{:S(2)}, u32[]{:S(2)}) %collective-permute-start.7) | collective-permute-done | bytes 524320 | tf_op jit(solution)/shard_map/ppermute | solution.py:265
  74.8 6.5 %collective-permute-done.10 = f32[1,2,256,256]{3,2,1,0:T(8,128)S(1)} collective-permute-done((f32[1,2,256,256]{3,2,1,0:T(8,128)S(1)}, f32[1,2,256,256]{3,2,1,0:T(8,128)S(1)}, u32[]{:S(2)}, u32[]{:S(2)}) %collective-permute-start.10) | collective-permute-done | bytes 524320 | tf_op jit(solution)/shard_map/ppermute | solution.py:265
  81.4 1.5 %collective-permute-start.11 = (f32[1,256,256]{2,1,0:T(8,128)S(1)}, f32[1,256,256]{2,1,0:T(8,128)S(1)}, u32[]{:S(2)}, u32[]{:S(2)}) collective-permute-start(f32[1,256,256]{2,1,0:T(8,128)S(1)} %fusion.6), channel_id=1, source_target_pairs={{0,16},{1,9},{2,18},{3,11},{4,20},{5,13},{6,22},{7,15},{8,24},{9,1... | collective-permute-start | bytes 786440 | tf_op jit(solution)/shard_map/ppermute | solution.py:265
  86.2 2.0 %collective-permute-start.13 = (f32[1,128,256]{2,1,0:T(8,128)S(1)}, f32[1,128,256]{2,1,0:T(8,128)S(1)}, u32[]{:S(2)}, u32[]{:S(2)}) collective-permute-start(f32[1,128,256]{2,1,0:T(8,128)S(1)} %slice.196), channel_id=1, source_target_pairs={{0,2},{1,3},{2,0},{3,1},{4,6},{5,7},{6,4},{7,5},{8,10},{9,11},{10,... | collective-permute-start | bytes 393224 | tf_op jit(solution)/shard_map/ppermute | solution.py:247
  89.6 4.6 %collective-permute-start.12 = (f32[2,256,512]{2,1,0:T(8,128)S(1)}, f32[2,256,512]{2,1,0:T(8,128)S(1)}, u32[]{:S(2)}, u32[]{:S(2)}) collective-permute-start(f32[2,256,512]{2,1,0:T(8,128)S(1)} %add_add_fusion), channel_id=1, source_target_pairs={{0,8},{8,16},{16,24},{1,9},{9,17},{17,25},{2,10},{10,18},{18,26},{... | collective-permute-start | bytes 3145736 | tf_op jit(solution)/shard_map/ppermute | solution.py:18
  95.5 3.0 %collective-permute-start.14 = (f32[1,128,256]{2,1,0:T(8,128)S(1)}, f32[1,128,256]{2,1,0:T(8,128)S(1)}, u32[]{:S(2)}, u32[]{:S(2)}) collective-permute-start(f32[1,128,256]{2,1,0:T(8,128)S(1)} %slice_add_fusion.12), channel_id=1, source_target_pairs={{0,4},{1,5},{2,6},{3,7},{4,0},{5,1},{6,2},{7,3},{8,12},{9,13},{10,... | collective-permute-start | bytes 393224 | tf_op jit(solution)/shard_map/ppermute | solution.py:247
  98.5 2.2 %collective-permute-done.18 = f32[1,128,256]{2,1,0:T(8,128)S(1)} collective-permute-done((f32[1,128,256]{2,1,0:T(8,128)S(1)}, f32[1,128,256]{2,1,0:T(8,128)S(1)}, u32[]{:S(2)}, u32[]{:S(2)}) %collective-permute-start.18) | collective-permute-done | bytes 131104 | tf_op jit(solution)/shard_map/ppermute | solution.py:247
  100.8 2.2 %collective-permute-start.19 = (f32[1,128,256]{2,1,0:T(8,128)S(1)}, f32[1,128,256]{2,1,0:T(8,128)S(1)}, u32[]{:S(2)}, u32[]{:S(2)}) collective-permute-start(f32[1,128,256]{2,1,0:T(8,128)S(1)} %slice_add_fusion.11), channel_id=1, source_target_pairs={{0,4},{1,5},{2,6},{3,7},{4,0},{5,1},{6,2},{7,3},{8,12},{9,13},{10,... | collective-permute-start | bytes 393224 | tf_op jit(solution)/shard_map/ppermute | solution.py:247
  103.0 3.2 %collective-permute-done.14 = f32[1,128,256]{2,1,0:T(8,128)S(1)} collective-permute-done((f32[1,128,256]{2,1,0:T(8,128)S(1)}, f32[1,128,256]{2,1,0:T(8,128)S(1)}, u32[]{:S(2)}, u32[]{:S(2)}) %collective-permute-start.14) | collective-permute-done | bytes 131104 | tf_op jit(solution)/shard_map/ppermute | solution.py:247
  106.3 2.8 %collective-permute-done.19 = f32[1,128,256]{2,1,0:T(8,128)S(1)} collective-permute-done((f32[1,128,256]{2,1,0:T(8,128)S(1)}, f32[1,128,256]{2,1,0:T(8,128)S(1)}, u32[]{:S(2)}, u32[]{:S(2)}) %collective-permute-start.19) | collective-permute-done | bytes 131104 | tf_op jit(solution)/shard_map/ppermute | solution.py:247
  109.1 2.8 %collective-permute-done.15 = f32[1,128,256]{2,1,0:T(8,128)S(1)} collective-permute-done((f32[1,128,256]{2,1,0:T(8,128)S(1)}, f32[1,128,256]{2,1,0:T(8,128)S(1)}, u32[]{:S(2)}, u32[]{:S(2)}) %collective-permute-start.15) | collective-permute-done | bytes 131104 | tf_op jit(solution)/shard_map/ppermute | solution.py:247
  111.9 1.7 %collective-permute-start.16 = (f32[1,256,256]{2,1,0:T(8,128)S(1)}, f32[1,256,256]{2,1,0:T(8,128)S(1)}, u32[]{:S(2)}, u32[]{:S(2)}) collective-permute-start(f32[1,256,256]{2,1,0:T(8,128)S(1)} %get-tuple-element.57), channel_id=1, source_target_pairs={{0,16},{1,9},{2,18},{3,11},{4,20},{5,13},{6,22},{7,15},{8,24},{9,1... | collective-permute-start | bytes 786440 | tf_op jit(solution)/shard_map/ppermute | solution.py:265
  113.7 3.9 %collective-permute-done.12 = f32[2,256,512]{2,1,0:T(8,128)S(1)} collective-permute-done((f32[2,256,512]{2,1,0:T(8,128)S(1)}, f32[2,256,512]{2,1,0:T(8,128)S(1)}, u32[]{:S(2)}, u32[]{:S(2)}) %collective-permute-start.12) | collective-permute-done | bytes 1048608 | tf_op jit(solution)/shard_map/ppermute | solution.py:18
  119.1 2.5 %collective-permute-start.21 = (f32[1,256,256]{2,1,0:T(8,128)S(1)}, f32[1,256,256]{2,1,0:T(8,128)S(1)}, u32[]{:S(2)}, u32[]{:S(2)}) collective-permute-start(f32[1,256,256]{2,1,0:T(8,128)S(1)} %maximum_add_fusion.1), channel_id=1, source_target_pairs={{0,16},{1,9},{2,18},{3,11},{4,20},{5,13},{6,22},{7,15},{8,24},{9,1... | collective-permute-start | bytes 786440 | tf_op jit(solution)/shard_map/ppermute | solution.py:265
  122.0 6.9 %collective-permute-done.21 = f32[1,256,256]{2,1,0:T(8,128)S(1)} collective-permute-done((f32[1,256,256]{2,1,0:T(8,128)S(1)}, f32[1,256,256]{2,1,0:T(8,128)S(1)}, u32[]{:S(2)}, u32[]{:S(2)}) %collective-permute-start.21) | collective-permute-done | bytes 262176 | tf_op jit(solution)/shard_map/ppermute | solution.py:265
  128.9 2.1 %collective-permute-start.22 = (f32[1,2,256,256]{3,2,1,0:T(8,128)S(1)}, f32[1,2,256,256]{3,2,1,0:T(8,128)S(1)}, u32[]{:S(2)}, u32[]{:S(2)}) collective-permute-start(f32[1,2,256,256]{3,2,1,0:T(8,128)S(1)} %pad_maximum_fusion.1.refs_2_), channel_id=1, source_target_pairs={{0,8},{1,17},{2,10},{3,19},{4,12},{5,21},{6,14},{7,23},{8,0},{9,25... | collective-permute-start | bytes 1572872 | tf_op jit(solution)/shard_map/ppermute | solution.py:265
  131.5 6.6 %collective-permute-done.22.refs_3_ = f32[1,2,256,256]{3,2,1,0:T(8,128)S(1)} collective-permute-done((f32[1,2,256,256]{3,2,1,0:T(8,128)S(1)}, f32[1,2,256,256]{3,2,1,0:T(8,128)S(1)}, u32[]{:S(2)}, u32[]{:S(2)}) %collective-permute-start.22) | collective-permute-done | bytes 524320 | tf_op jit(solution)/shard_map/ppermute | solution.py:265
  140.1 2.8 %shard_map.106 = f32[2,8,256,256]{3,2,1,0:T(8,128)} custom-call(s32[6]{0:T(128)S(1)} %stack.37.bit_ref, f32[1,2,256,256]{3,2,1,0:T(8,128)S(1)} %pad_maximum_fusion.refs_0_, f32[1,2,256,256]{3,2,1,0:T(8,128)S(1)} %collective-permute-done.17.refs_1_, f32[1,2,256,256]{3,2,1,0:T(8,128)S(1)} %pad_maximum_fusion.1.refs_2_, ...), custom_call_target="tpu_custom_call" | custom-call | tf_op jit(solution)/shard_map/pallas_call | solution.py:293
  (81 shorter events, 21.8 us)
Async XLA Ops:
  2.1 17.7 %collective-permute-start.1 = (f32[2,256,256]{2,1,0:T(8,128)S(1)}, f32[2,256,256]{2,1,0:T(8,128)S(1)}, u32[]{:S(2)}, u32[]{:S(2)}) collective-permute-start(f32[2,256,256]{2,1,0:T(8,128)S(1)} %get-tuple-element.55), channel_id=1, source_target_pairs={{8,0},{16,8},{24,16},{9,1},{17,9},{25,17},{10,2},{18,10},{26,18},{... | collective-permute-start | bytes 1572872 | tf_op jit(solution)/shard_map/ppermute | solution.py:18
  3.7 26.6 %collective-permute-start = (f32[2,512,256]{2,1,0:T(8,128)S(1)}, f32[2,512,256]{2,1,0:T(8,128)}, u32[]{:S(2)}, u32[]{:S(2)}) collective-permute-start(f32[2,512,256]{2,1,0:T(8,128)S(1)} %slice.153), channel_id=1, source_target_pairs={{1,0},{2,1},{3,2},{4,3},{5,4},{6,5},{7,6},{9,8},{10,9},{11,10},{12... | collective-permute-start | bytes 3145736 | tf_op jit(solution)/shard_map/ppermute | solution.py:18
  5.0 25.3 %collective-permute-start.2 = (f32[2,256,256]{2,1,0:T(8,128)S(1)}, f32[2,256,256]{2,1,0:T(8,128)S(1)}, u32[]{:S(2)}, u32[]{:S(2)}) collective-permute-start(f32[2,256,256]{2,1,0:T(8,128)S(1)} %get-tuple-element.54), channel_id=1, source_target_pairs={{8,0},{16,8},{24,16},{9,1},{17,9},{25,17},{10,2},{18,10},{26,18},{... | collective-permute-start | bytes 1572872 | tf_op jit(solution)/shard_map/ppermute | solution.py:18
  19.9 10.4 %collective-permute-start.3 = (f32[2,256,256]{2,1,0:T(8,128)S(1)}, f32[2,256,256]{2,1,0:T(8,128)S(1)}, u32[]{:S(2)}, u32[]{:S(2)}) collective-permute-start(f32[2,256,256]{2,1,0:T(8,128)S(1)} %collective-permute-done.1.below0), channel_id=1, source_target_pairs={{1,0},{2,1},{3,2},{4,3},{5,4},{6,5},{7,6},{9,8},{10,9},{11,10},{12... | collective-permute-start | bytes 1572872 | tf_op jit(solution)/shard_map/ppermute | solution.py:18
  61.4 21.6 %collective-permute-start.4 = (f32[2,512,256]{2,1,0:T(8,128)S(1)}, f32[2,512,256]{2,1,0:T(8,128)S(1)}, u32[]{:S(2)}, u32[]{:S(2)}) collective-permute-start(f32[2,512,256]{2,1,0:T(8,128)S(1)} %get-tuple-element.47), channel_id=1, source_target_pairs={{0,1},{1,2},{2,3},{3,4},{4,5},{5,6},{6,7},{8,9},{9,10},{10,11},{11... | collective-permute-start | bytes 3145736 | tf_op jit(solution)/shard_map/ppermute | solution.py:18
  63.9 9.6 %collective-permute-start.7 = (f32[1,2,256,256]{3,2,1,0:T(8,128)S(1)}, f32[1,2,256,256]{3,2,1,0:T(8,128)S(1)}, u32[]{:S(2)}, u32[]{:S(2)}) collective-permute-start(f32[1,2,256,256]{3,2,1,0:T(8,128)S(1)} %slice_add_fusion.2), channel_id=1, source_target_pairs={{0,8},{1,17},{2,10},{3,19},{4,12},{5,21},{6,14},{7,23},{8,0},{9,25... | collective-permute-start | bytes 1572872 | tf_op jit(solution)/shard_map/ppermute | solution.py:265
  67.5 13.8 %collective-permute-start.10 = (f32[1,2,256,256]{3,2,1,0:T(8,128)S(1)}, f32[1,2,256,256]{3,2,1,0:T(8,128)S(1)}, u32[]{:S(2)}, u32[]{:S(2)}) collective-permute-start(f32[1,2,256,256]{3,2,1,0:T(8,128)S(1)} %slice_add_fusion.1), channel_id=1, source_target_pairs={{0,8},{1,17},{2,10},{3,19},{4,12},{5,21},{6,14},{7,23},{8,0},{9,25... | collective-permute-start | bytes 1572872 | tf_op jit(solution)/shard_map/ppermute | solution.py:265
  68.9 14.0 %collective-permute-start.5 = (f32[2,256,256]{2,1,0:T(8,128)S(1)}, f32[2,256,256]{2,1,0:T(8,128)S(1)}, u32[]{:S(2)}, u32[]{:S(2)}) collective-permute-start(f32[2,256,256]{2,1,0:T(8,128)S(1)} %get-tuple-element.49), channel_id=1, source_target_pairs={{0,1},{1,2},{2,3},{3,4},{4,5},{5,6},{6,7},{8,9},{9,10},{10,11},{11... | collective-permute-start | bytes 1572872 | tf_op jit(solution)/shard_map/ppermute | solution.py:18
  73.6 11.1 %collective-permute-start.8 = (f32[1,256,256]{2,1,0:T(8,128)S(1)}, f32[1,256,256]{2,1,0:T(8,128)S(1)}, u32[]{:S(2)}, u32[]{:S(2)}) collective-permute-start(f32[1,256,256]{2,1,0:T(8,128)S(1)} %fusion.7), channel_id=1, source_target_pairs={{0,16},{1,9},{2,18},{3,11},{4,20},{5,13},{6,22},{7,15},{8,24},{9,1... | collective-permute-start | bytes 786440 | tf_op jit(solution)/shard_map/ppermute | solution.py:265
  81.4 6.8 %collective-permute-start.11 = (f32[1,256,256]{2,1,0:T(8,128)S(1)}, f32[1,256,256]{2,1,0:T(8,128)S(1)}, u32[]{:S(2)}, u32[]{:S(2)}) collective-permute-start(f32[1,256,256]{2,1,0:T(8,128)S(1)} %fusion.6), channel_id=1, source_target_pairs={{0,16},{1,9},{2,18},{3,11},{4,20},{5,13},{6,22},{7,15},{8,24},{9,1... | collective-permute-start | bytes 786440 | tf_op jit(solution)/shard_map/ppermute | solution.py:265
  86.2 9.4 %collective-permute-start.13 = (f32[1,128,256]{2,1,0:T(8,128)S(1)}, f32[1,128,256]{2,1,0:T(8,128)S(1)}, u32[]{:S(2)}, u32[]{:S(2)}) collective-permute-start(f32[1,128,256]{2,1,0:T(8,128)S(1)} %slice.196), channel_id=1, source_target_pairs={{0,2},{1,3},{2,0},{3,1},{4,6},{5,7},{6,4},{7,5},{8,10},{9,11},{10,... | collective-permute-start | bytes 393224 | tf_op jit(solution)/shard_map/ppermute | solution.py:247
  89.6 27.9 %collective-permute-start.12 = (f32[2,256,512]{2,1,0:T(8,128)S(1)}, f32[2,256,512]{2,1,0:T(8,128)S(1)}, u32[]{:S(2)}, u32[]{:S(2)}) collective-permute-start(f32[2,256,512]{2,1,0:T(8,128)S(1)} %add_add_fusion), channel_id=1, source_target_pairs={{0,8},{8,16},{16,24},{1,9},{9,17},{17,25},{2,10},{10,18},{18,26},{... | collective-permute-start | bytes 3145736 | tf_op jit(solution)/shard_map/ppermute | solution.py:18
  94.3 6.5 %collective-permute-start.18 = (f32[1,128,256]{2,1,0:T(8,128)S(1)}, f32[1,128,256]{2,1,0:T(8,128)S(1)}, u32[]{:S(2)}, u32[]{:S(2)}) collective-permute-start(f32[1,128,256]{2,1,0:T(8,128)S(1)} %slice.200), channel_id=1, source_target_pairs={{0,2},{1,3},{2,0},{3,1},{4,6},{5,7},{6,4},{7,5},{8,10},{9,11},{10,... | collective-permute-start | bytes 393224 | tf_op jit(solution)/shard_map/ppermute | solution.py:247
  95.5 10.6 %collective-permute-start.14 = (f32[1,128,256]{2,1,0:T(8,128)S(1)}, f32[1,128,256]{2,1,0:T(8,128)S(1)}, u32[]{:S(2)}, u32[]{:S(2)}) collective-permute-start(f32[1,128,256]{2,1,0:T(8,128)S(1)} %slice_add_fusion.12), channel_id=1, source_target_pairs={{0,4},{1,5},{2,6},{3,7},{4,0},{5,1},{6,2},{7,3},{8,12},{9,13},{10,... | collective-permute-start | bytes 393224 | tf_op jit(solution)/shard_map/ppermute | solution.py:247
  100.8 8.2 %collective-permute-start.19 = (f32[1,128,256]{2,1,0:T(8,128)S(1)}, f32[1,128,256]{2,1,0:T(8,128)S(1)}, u32[]{:S(2)}, u32[]{:S(2)}) collective-permute-start(f32[1,128,256]{2,1,0:T(8,128)S(1)} %slice_add_fusion.11), channel_id=1, source_target_pairs={{0,4},{1,5},{2,6},{3,7},{4,0},{5,1},{6,2},{7,3},{8,12},{9,13},{10,... | collective-permute-start | bytes 393224 | tf_op jit(solution)/shard_map/ppermute | solution.py:247
  106.2 5.7 %collective-permute-start.15 = (f32[1,128,256]{2,1,0:T(8,128)S(1)}, f32[1,128,256]{2,1,0:T(8,128)S(1)}, u32[]{:S(2)}, u32[]{:S(2)}) collective-permute-start(f32[1,128,256]{2,1,0:T(8,128)S(1)} %add.214), channel_id=1, source_target_pairs={{0,2},{1,3},{2,0},{3,1},{4,6},{5,7},{6,4},{7,5},{8,10},{9,11},{10,... | collective-permute-start | bytes 393224 | tf_op jit(solution)/shard_map/ppermute | solution.py:247
  109.0 10.0 %collective-permute-start.20 = (f32[1,128,256]{2,1,0:T(8,128)S(1)}, f32[1,128,256]{2,1,0:T(8,128)S(1)}, u32[]{:S(2)}, u32[]{:S(2)}) collective-permute-start(f32[1,128,256]{2,1,0:T(8,128)S(1)} %add.220), channel_id=1, source_target_pairs={{0,2},{1,3},{2,0},{3,1},{4,6},{5,7},{6,4},{7,5},{8,10},{9,11},{10,... | collective-permute-start | bytes 393224 | tf_op jit(solution)/shard_map/ppermute | solution.py:247
  111.9 9.7 %collective-permute-start.16 = (f32[1,256,256]{2,1,0:T(8,128)S(1)}, f32[1,256,256]{2,1,0:T(8,128)S(1)}, u32[]{:S(2)}, u32[]{:S(2)}) collective-permute-start(f32[1,256,256]{2,1,0:T(8,128)S(1)} %get-tuple-element.57), channel_id=1, source_target_pairs={{0,16},{1,9},{2,18},{3,11},{4,20},{5,13},{6,22},{7,15},{8,24},{9,1... | collective-permute-start | bytes 786440 | tf_op jit(solution)/shard_map/ppermute | solution.py:265
  119.1 9.7 %collective-permute-start.21 = (f32[1,256,256]{2,1,0:T(8,128)S(1)}, f32[1,256,256]{2,1,0:T(8,128)S(1)}, u32[]{:S(2)}, u32[]{:S(2)}) collective-permute-start(f32[1,256,256]{2,1,0:T(8,128)S(1)} %maximum_add_fusion.1), channel_id=1, source_target_pairs={{0,16},{1,9},{2,18},{3,11},{4,20},{5,13},{6,22},{7,15},{8,24},{9,1... | collective-permute-start | bytes 786440 | tf_op jit(solution)/shard_map/ppermute | solution.py:265
  121.7 9.3 %collective-permute-start.17 = (f32[1,2,256,256]{3,2,1,0:T(8,128)S(1)}, f32[1,2,256,256]{3,2,1,0:T(8,128)S(1)}, u32[]{:S(2)}, u32[]{:S(2)}) collective-permute-start(f32[1,2,256,256]{3,2,1,0:T(8,128)S(1)} %pad_maximum_fusion.refs_0_), channel_id=1, source_target_pairs={{0,8},{1,17},{2,10},{3,19},{4,12},{5,21},{6,14},{7,23},{8,0},{9,25... | collective-permute-start | bytes 1572872 | tf_op jit(solution)/shard_map/ppermute | solution.py:265
  128.9 9.3 %collective-permute-start.22 = (f32[1,2,256,256]{3,2,1,0:T(8,128)S(1)}, f32[1,2,256,256]{3,2,1,0:T(8,128)S(1)}, u32[]{:S(2)}, u32[]{:S(2)}) collective-permute-start(f32[1,2,256,256]{3,2,1,0:T(8,128)S(1)} %pad_maximum_fusion.1.refs_2_), channel_id=1, source_target_pairs={{0,8},{1,17},{2,10},{3,19},{4,12},{5,21},{6,14},{7,23},{8,0},{9,25... | collective-permute-start | bytes 1572872 | tf_op jit(solution)/shard_map/ppermute | solution.py:265
  131.0 7.7 %collective-permute-start.23 = (f32[1,2,256,256]{3,2,1,0:T(8,128)S(1)}, f32[1,2,256,256]{3,2,1,0:T(8,128)S(1)}, u32[]{:S(2)}, u32[]{:S(2)}) collective-permute-start(f32[1,2,256,256]{3,2,1,0:T(8,128)S(1)} %pad_maximum_fusion.refs_0_), channel_id=1, source_target_pairs={{0,1},{1,0},{2,3},{3,2},{4,5},{5,4},{6,7},{7,6},{8,9},{9,8},{10,11... | collective-permute-start | bytes 1572872 | tf_op jit(solution)/shard_map/ppermute | solution.py:247
  131.0 7.7 %collective-permute-start.24 = (f32[1,2,256,256]{3,2,1,0:T(8,128)S(1)}, f32[1,2,256,256]{3,2,1,0:T(8,128)S(1)}, u32[]{:S(2)}, u32[]{:S(2)}) collective-permute-start(f32[1,2,256,256]{3,2,1,0:T(8,128)S(1)} %collective-permute-done.17.refs_1_), channel_id=1, source_target_pairs={{0,1},{1,0},{2,3},{3,2},{4,5},{5,4},{6,7},{7,6},{8,9},{9,8},{10,11... | collective-permute-start | bytes 1572872 | tf_op jit(solution)/shard_map/ppermute | solution.py:247
  131.5 7.3 %collective-permute-start.25 = (f32[1,2,256,256]{3,2,1,0:T(8,128)S(1)}, f32[1,2,256,256]{3,2,1,0:T(8,128)S(1)}, u32[]{:S(2)}, u32[]{:S(2)}) collective-permute-start(f32[1,2,256,256]{3,2,1,0:T(8,128)S(1)} %pad_maximum_fusion.1.refs_2_), channel_id=1, source_target_pairs={{0,1},{1,0},{2,3},{3,2},{4,5},{5,4},{6,7},{7,6},{8,9},{9,8},{10,11... | collective-permute-start | bytes 1572872 | tf_op jit(solution)/shard_map/ppermute | solution.py:247
  (11 other events, 140.7 us)

commit v4 on v3

--- a/solution.py
+++ b/solution.py
@@ -277,7 +277,7 @@
         totals.append(keep[:one, 0] + came[:one, 0] + came1[:, 0] + came2)
     from_above = passed_along(below_grad, "row", 1)
     own = []
-    totals[0] = after(totals[0], from_left)
+    totals[1] = after(totals[1], from_left)
     for number, total in enumerate(totals):
         total = total[:, :half] + swap(total[:, half:], third)
         for where in rest:

time: 144 us -> 143 us (level)
  no operation moved by 1% of the time
where the time goes in v4:
time: 143 us
  waiting for transfers between devices  58.6 us (41%)
  starting transfers between devices  37.3 us (26%)
  Pallas kernels  34.9 us (24%)
  local copies, waits for them, and re-layouts  5.88 us (4%)
  between operations  3.92 us (3%)
  other arithmetic  2.45 us (2%)
    pallas_call x1, Pallas kernels, shards(): pl.pallas_call(kernel, out_shape=(jax.ShapeDtypeStruct((2, rows, cols), f...  29.3 us
    ppermute x7, waiting for transfers between devices, passed_along(): return lax.ppermute(array, axis, pairs)  23.7 us
    ppermute x8, waiting for transfers between devices, hop(): return lax.ppermute(array, ('row', 'col'), pairs)  23.4 us
    ppermute x7, starting transfers between devices, passed_along(): return lax.ppermute(array, axis, pairs)  13.6 us
    ppermute x8, starting transfers between devices, hop(): return lax.ppermute(array, ('row', 'col'), pairs)  13 us
    ppermute x12, waiting for transfers between devices, swap(): lax.ppermute(array, axis, [(i, i ^ 1 << bit) for i in range(lax.axis_size...  11.5 us
    ppermute x12, starting transfers between devices, swap(): lax.ppermute(array, axis, [(i, i ^ 1 << bit) for i in range(lax.axis_size...  10.7 us
  transfers between devices with their start and end apart: 27, of which 12 were waited for; matrix products, arithmetic and copies ran while one was open for 4% of the time, Pallas kernels for 2%

profile of v4, /device:TPU:0, one launch (start us, length us, event | category | flops | bytes accessed | tf_op | source)
XLA Modules:
  0.0 143.1 jit_solution(12260699116702524557)
XLA Ops:
  6.3 13.6 %collective-permute-done.1.below0 = f32[2,256,256]{2,1,0:T(8,128)S(1)} collective-permute-done((f32[2,256,256]{2,1,0:T(8,128)S(1)}, f32[2,256,256]{2,1,0:T(8,128)S(1)}, u32[]{:S(2)}, u32[]{:S(2)}) %collective-permute-start.1) | collective-permute-done | bytes 524320 | tf_op jit(solution)/shard_map/ppermute | solution.py:18
  21.2 2.8 %shard_map.104.root_in = f32[2,2,128,256]{3,2,1,0:T(8,128)} custom-call(f32[2,256,256]{2,1,0:T(8,128)} %intensity.1, bf16[2,256,256]{2,1,0:T(8,128)(2,1)} %constant.97.clone.orders), custom_call_target="tpu_custom_call" | custom-call | tf_op jit(solution)/shard_map/pallas_call | solution.py:324
  24.0 6.2 %collective-permute-done.2.below1 = f32[2,256,256]{2,1,0:T(8,128)S(1)} collective-permute-done((f32[2,256,256]{2,1,0:T(8,128)S(1)}, f32[2,256,256]{2,1,0:T(8,128)S(1)}, u32[]{:S(2)}, u32[]{:S(2)}) %collective-permute-start.2) | collective-permute-done | bytes 524320 | tf_op jit(solution)/shard_map/ppermute | solution.py:18
  31.3 29.3 %shard_map.105 = (f32[2,512,512]{2,1,0:T(8,128)}, f32[2,512,256]{2,1,0:T(8,128)S(1)}, f32[2,256,512]{2,1,0:T(8,128)S(1)}, f32[2,256,256]{2,1,0:T(8,128)S(1)}, f3...) custom-call(s32[2]{0:T(128)S(1)} %copy-done.1, ...), custom_call_target="tpu_custom_call" | custom-call | tf_op jit(solution)/shard_map/pallas_call | solution.py:338
  61.4 2.4 %collective-permute-start.4 = (f32[2,512,256]{2,1,0:T(8,128)S(1)}, f32[2,512,256]{2,1,0:T(8,128)S(1)}, u32[]{:S(2)}, u32[]{:S(2)}) collective-permute-start(f32[2,512,256]{2,1,0:T(8,128)S(1)} %get-tuple-element.47), channel_id=1, source_target_pairs={{0,1},{1,2},{2,3},{3,4},{4,5},{5,6},{6,7},{8,9},{9,10},{10,11},{11... | collective-permute-start | bytes 3145736 | tf_op jit(solution)/shard_map/ppermute | solution.py:18
  63.9 2.5 %collective-permute-start.7 = (f32[1,2,256,256]{3,2,1,0:T(8,128)S(1)}, f32[1,2,256,256]{3,2,1,0:T(8,128)S(1)}, u32[]{:S(2)}, u32[]{:S(2)}) collective-permute-start(f32[1,2,256,256]{3,2,1,0:T(8,128)S(1)} %slice_add_fusion.2), channel_id=1, source_target_pairs={{0,8},{1,17},{2,10},{3,19},{4,12},{5,21},{6,14},{7,23},{8,0},{9,25... | collective-permute-start | bytes 1572872 | tf_op jit(solution)/shard_map/ppermute | solution.py:265
  70.2 3.3 %collective-permute-done.7 = f32[1,2,256,256]{3,2,1,0:T(8,128)S(1)} collective-permute-done((f32[1,2,256,256]{3,2,1,0:T(8,128)S(1)}, f32[1,2,256,256]{3,2,1,0:T(8,128)S(1)}, u32[]{:S(2)}, u32[]{:S(2)}) %collective-permute-start.7) | collective-permute-done | bytes 524320 | tf_op jit(solution)/shard_map/ppermute | solution.py:265
  74.8 6.5 %collective-permute-done.10 = f32[1,2,256,256]{3,2,1,0:T(8,128)S(1)} collective-permute-done((f32[1,2,256,256]{3,2,1,0:T(8,128)S(1)}, f32[1,2,256,256]{3,2,1,0:T(8,128)S(1)}, u32[]{:S(2)}, u32[]{:S(2)}) %collective-permute-start.10) | collective-permute-done | bytes 524320 | tf_op jit(solution)/shard_map/ppermute | solution.py:265
  81.4 1.5 %collective-permute-start.11 = (f32[1,256,256]{2,1,0:T(8,128)S(1)}, f32[1,256,256]{2,1,0:T(8,128)S(1)}, u32[]{:S(2)}, u32[]{:S(2)}) collective-permute-start(f32[1,256,256]{2,1,0:T(8,128)S(1)} %fusion.6), channel_id=1, source_target_pairs={{0,16},{1,9},{2,18},{3,11},{4,20},{5,13},{6,22},{7,15},{8,24},{9,1... | collective-permute-start | bytes 786440 | tf_op jit(solution)/shard_map/ppermute | solution.py:265
  86.1 2.0 %collective-permute-start.13 = (f32[1,128,256]{2,1,0:T(8,128)S(1)}, f32[1,128,256]{2,1,0:T(8,128)S(1)}, u32[]{:S(2)}, u32[]{:S(2)}) collective-permute-start(f32[1,128,256]{2,1,0:T(8,128)S(1)} %slice.195), channel_id=1, source_target_pairs={{0,2},{1,3},{2,0},{3,1},{4,6},{5,7},{6,4},{7,5},{8,10},{9,11},{10,... | collective-permute-start | bytes 393224 | tf_op jit(solution)/shard_map/ppermute | solution.py:247
  89.6 4.6 %collective-permute-start.12 = (f32[2,256,512]{2,1,0:T(8,128)S(1)}, f32[2,256,512]{2,1,0:T(8,128)S(1)}, u32[]{:S(2)}, u32[]{:S(2)}) collective-permute-start(f32[2,256,512]{2,1,0:T(8,128)S(1)} %add_add_fusion), channel_id=1, source_target_pairs={{0,8},{8,16},{16,24},{1,9},{9,17},{17,25},{2,10},{10,18},{18,26},{... | collective-permute-start | bytes 3145736 | tf_op jit(solution)/shard_map/ppermute | solution.py:18
  95.5 3.0 %collective-permute-start.14 = (f32[1,128,256]{2,1,0:T(8,128)S(1)}, f32[1,128,256]{2,1,0:T(8,128)S(1)}, u32[]{:S(2)}, u32[]{:S(2)}) collective-permute-start(f32[1,128,256]{2,1,0:T(8,128)S(1)} %slice_add_fusion.12), channel_id=1, source_target_pairs={{0,4},{1,5},{2,6},{3,7},{4,0},{5,1},{6,2},{7,3},{8,12},{9,13},{10,... | collective-permute-start | bytes 393224 | tf_op jit(solution)/shard_map/ppermute | solution.py:247
  98.5 2.2 %collective-permute-done.18 = f32[1,128,256]{2,1,0:T(8,128)S(1)} collective-permute-done((f32[1,128,256]{2,1,0:T(8,128)S(1)}, f32[1,128,256]{2,1,0:T(8,128)S(1)}, u32[]{:S(2)}, u32[]{:S(2)}) %collective-permute-start.18) | collective-permute-done | bytes 131104 | tf_op jit(solution)/shard_map/ppermute | solution.py:247
  100.8 2.1 %collective-permute-start.19 = (f32[1,128,256]{2,1,0:T(8,128)S(1)}, f32[1,128,256]{2,1,0:T(8,128)S(1)}, u32[]{:S(2)}, u32[]{:S(2)}) collective-permute-start(f32[1,128,256]{2,1,0:T(8,128)S(1)} %slice_add_fusion.11), channel_id=1, source_target_pairs={{0,4},{1,5},{2,6},{3,7},{4,0},{5,1},{6,2},{7,3},{8,12},{9,13},{10,... | collective-permute-start | bytes 393224 | tf_op jit(solution)/shard_map/ppermute | solution.py:247
  102.9 3.3 %collective-permute-done.14 = f32[1,128,256]{2,1,0:T(8,128)S(1)} collective-permute-done((f32[1,128,256]{2,1,0:T(8,128)S(1)}, f32[1,128,256]{2,1,0:T(8,128)S(1)}, u32[]{:S(2)}, u32[]{:S(2)}) %collective-permute-start.14) | collective-permute-done | bytes 131104 | tf_op jit(solution)/shard_map/ppermute | solution.py:247
  107.2 1.8 %collective-permute-done.19 = f32[1,128,256]{2,1,0:T(8,128)S(1)} collective-permute-done((f32[1,128,256]{2,1,0:T(8,128)S(1)}, f32[1,128,256]{2,1,0:T(8,128)S(1)}, u32[]{:S(2)}, u32[]{:S(2)}) %collective-permute-start.19) | collective-permute-done | bytes 131104 | tf_op jit(solution)/shard_map/ppermute | solution.py:247
  109.2 2.8 %collective-permute-done.15 = f32[1,128,256]{2,1,0:T(8,128)S(1)} collective-permute-done((f32[1,128,256]{2,1,0:T(8,128)S(1)}, f32[1,128,256]{2,1,0:T(8,128)S(1)}, u32[]{:S(2)}, u32[]{:S(2)}) %collective-permute-start.15) | collective-permute-done | bytes 131104 | tf_op jit(solution)/shard_map/ppermute | solution.py:247
  112.1 1.5 %collective-permute-start.16 = (f32[1,256,256]{2,1,0:T(8,128)S(1)}, f32[1,256,256]{2,1,0:T(8,128)S(1)}, u32[]{:S(2)}, u32[]{:S(2)}) collective-permute-start(f32[1,256,256]{2,1,0:T(8,128)S(1)} %get-tuple-element.57), channel_id=1, source_target_pairs={{0,16},{1,9},{2,18},{3,11},{4,20},{5,13},{6,22},{7,15},{8,24},{9,1... | collective-permute-start | bytes 786440 | tf_op jit(solution)/shard_map/ppermute | solution.py:265
  113.6 3.9 %collective-permute-done.12 = f32[2,256,512]{2,1,0:T(8,128)S(1)} collective-permute-done((f32[2,256,512]{2,1,0:T(8,128)S(1)}, f32[2,256,512]{2,1,0:T(8,128)S(1)}, u32[]{:S(2)}, u32[]{:S(2)}) %collective-permute-start.12) | collective-permute-done | bytes 1048608 | tf_op jit(solution)/shard_map/ppermute | solution.py:18
  119.1 2.5 %collective-permute-start.21 = (f32[1,256,256]{2,1,0:T(8,128)S(1)}, f32[1,256,256]{2,1,0:T(8,128)S(1)}, u32[]{:S(2)}, u32[]{:S(2)}) collective-permute-start(f32[1,256,256]{2,1,0:T(8,128)S(1)} %maximum_add_fusion.1), channel_id=1, source_target_pairs={{0,16},{1,9},{2,18},{3,11},{4,20},{5,13},{6,22},{7,15},{8,24},{9,1... | collective-permute-start | bytes 786440 | tf_op jit(solution)/shard_map/ppermute | solution.py:265
  121.9 6.9 %collective-permute-done.21 = f32[1,256,256]{2,1,0:T(8,128)S(1)} collective-permute-done((f32[1,256,256]{2,1,0:T(8,128)S(1)}, f32[1,256,256]{2,1,0:T(8,128)S(1)}, u32[]{:S(2)}, u32[]{:S(2)}) %collective-permute-start.21) | collective-permute-done | bytes 262176 | tf_op jit(solution)/shard_map/ppermute | solution.py:265
  128.9 2.1 %collective-permute-start.22 = (f32[1,2,256,256]{3,2,1,0:T(8,128)S(1)}, f32[1,2,256,256]{3,2,1,0:T(8,128)S(1)}, u32[]{:S(2)}, u32[]{:S(2)}) collective-permute-start(f32[1,2,256,256]{3,2,1,0:T(8,128)S(1)} %pad_maximum_fusion.1.refs_2_), channel_id=1, source_target_pairs={{0,8},{1,17},{2,10},{3,19},{4,12},{5,21},{6,14},{7,23},{8,0},{9,25... | collective-permute-start | bytes 1572872 | tf_op jit(solution)/shard_map/ppermute | solution.py:265
  131.5 6.6 %collective-permute-done.22.refs_3_ = f32[1,2,256,256]{3,2,1,0:T(8,128)S(1)} collective-permute-done((f32[1,2,256,256]{3,2,1,0:T(8,128)S(1)}, f32[1,2,256,256]{3,2,1,0:T(8,128)S(1)}, u32[]{:S(2)}, u32[]{:S(2)}) %collective-permute-start.22) | collective-permute-done | bytes 524320 | tf_op jit(solution)/shard_map/ppermute | solution.py:265
  140.1 2.8 %shard_map.106 = f32[2,8,256,256]{3,2,1,0:T(8,128)} custom-call(s32[6]{0:T(128)S(1)} %stack.37.bit_ref, f32[1,2,256,256]{3,2,1,0:T(8,128)S(1)} %pad_maximum_fusion.refs_0_, f32[1,2,256,256]{3,2,1,0:T(8,128)S(1)} %collective-permute-done.17.refs_1_, f32[1,2,256,256]{3,2,1,0:T(8,128)S(1)} %pad_maximum_fusion.1.refs_2_, ...), custom_call_target="tpu_custom_call" | custom-call | tf_op jit(solution)/shard_map/pallas_call | solution.py:293
  (81 shorter events, 22.7 us)
Async XLA Ops:
  2.1 17.7 %collective-permute-start.1 = (f32[2,256,256]{2,1,0:T(8,128)S(1)}, f32[2,256,256]{2,1,0:T(8,128)S(1)}, u32[]{:S(2)}, u32[]{:S(2)}) collective-permute-start(f32[2,256,256]{2,1,0:T(8,128)S(1)} %get-tuple-element.55), channel_id=1, source_target_pairs={{8,0},{16,8},{24,16},{9,1},{17,9},{25,17},{10,2},{18,10},{26,18},{... | collective-permute-start | bytes 1572872 | tf_op jit(solution)/shard_map/ppermute | solution.py:18
  3.7 26.6 %collective-permute-start = (f32[2,512,256]{2,1,0:T(8,128)S(1)}, f32[2,512,256]{2,1,0:T(8,128)}, u32[]{:S(2)}, u32[]{:S(2)}) collective-permute-start(f32[2,512,256]{2,1,0:T(8,128)S(1)} %slice.153), channel_id=1, source_target_pairs={{1,0},{2,1},{3,2},{4,3},{5,4},{6,5},{7,6},{9,8},{10,9},{11,10},{12... | collective-permute-start | bytes 3145736 | tf_op jit(solution)/shard_map/ppermute | solution.py:18
  5.0 25.3 %collective-permute-start.2 = (f32[2,256,256]{2,1,0:T(8,128)S(1)}, f32[2,256,256]{2,1,0:T(8,128)S(1)}, u32[]{:S(2)}, u32[]{:S(2)}) collective-permute-start(f32[2,256,256]{2,1,0:T(8,128)S(1)} %get-tuple-element.54), channel_id=1, source_target_pairs={{8,0},{16,8},{24,16},{9,1},{17,9},{25,17},{10,2},{18,10},{26,18},{... | collective-permute-start | bytes 1572872 | tf_op jit(solution)/shard_map/ppermute | solution.py:18
  19.9 10.4 %collective-permute-start.3 = (f32[2,256,256]{2,1,0:T(8,128)S(1)}, f32[2,256,256]{2,1,0:T(8,128)S(1)}, u32[]{:S(2)}, u32[]{:S(2)}) collective-permute-start(f32[2,256,256]{2,1,0:T(8,128)S(1)} %collective-permute-done.1.below0), channel_id=1, source_target_pairs={{1,0},{2,1},{3,2},{4,3},{5,4},{6,5},{7,6},{9,8},{10,9},{11,10},{12... | collective-permute-start | bytes 1572872 | tf_op jit(solution)/shard_map/ppermute | solution.py:18
  61.4 21.6 %collective-permute-start.4 = (f32[2,512,256]{2,1,0:T(8,128)S(1)}, f32[2,512,256]{2,1,0:T(8,128)S(1)}, u32[]{:S(2)}, u32[]{:S(2)}) collective-permute-start(f32[2,512,256]{2,1,0:T(8,128)S(1)} %get-tuple-element.47), channel_id=1, source_target_pairs={{0,1},{1,2},{2,3},{3,4},{4,5},{5,6},{6,7},{8,9},{9,10},{10,11},{11... | collective-permute-start | bytes 3145736 | tf_op jit(solution)/shard_map/ppermute | solution.py:18
  63.9 9.6 %collective-permute-start.7 = (f32[1,2,256,256]{3,2,1,0:T(8,128)S(1)}, f32[1,2,256,256]{3,2,1,0:T(8,128)S(1)}, u32[]{:S(2)}, u32[]{:S(2)}) collective-permute-start(f32[1,2,256,256]{3,2,1,0:T(8,128)S(1)} %slice_add_fusion.2), channel_id=1, source_target_pairs={{0,8},{1,17},{2,10},{3,19},{4,12},{5,21},{6,14},{7,23},{8,0},{9,25... | collective-permute-start | bytes 1572872 | tf_op jit(solution)/shard_map/ppermute | solution.py:265
  67.5 13.8 %collective-permute-start.10 = (f32[1,2,256,256]{3,2,1,0:T(8,128)S(1)}, f32[1,2,256,256]{3,2,1,0:T(8,128)S(1)}, u32[]{:S(2)}, u32[]{:S(2)}) collective-permute-start(f32[1,2,256,256]{3,2,1,0:T(8,128)S(1)} %slice_add_fusion.1), channel_id=1, source_target_pairs={{0,8},{1,17},{2,10},{3,19},{4,12},{5,21},{6,14},{7,23},{8,0},{9,25... | collective-permute-start | bytes 1572872 | tf_op jit(solution)/shard_map/ppermute | solution.py:265
  68.9 13.9 %collective-permute-start.5 = (f32[2,256,256]{2,1,0:T(8,128)S(1)}, f32[2,256,256]{2,1,0:T(8,128)S(1)}, u32[]{:S(2)}, u32[]{:S(2)}) collective-permute-start(f32[2,256,256]{2,1,0:T(8,128)S(1)} %get-tuple-element.49), channel_id=1, source_target_pairs={{0,1},{1,2},{2,3},{3,4},{4,5},{5,6},{6,7},{8,9},{9,10},{10,11},{11... | collective-permute-start | bytes 1572872 | tf_op jit(solution)/shard_map/ppermute | solution.py:18
  73.6 11.1 %collective-permute-start.8 = (f32[1,256,256]{2,1,0:T(8,128)S(1)}, f32[1,256,256]{2,1,0:T(8,128)S(1)}, u32[]{:S(2)}, u32[]{:S(2)}) collective-permute-start(f32[1,256,256]{2,1,0:T(8,128)S(1)} %fusion.7), channel_id=1, source_target_pairs={{0,16},{1,9},{2,18},{3,11},{4,20},{5,13},{6,22},{7,15},{8,24},{9,1... | collective-permute-start | bytes 786440 | tf_op jit(solution)/shard_map/ppermute | solution.py:265
  81.4 6.8 %collective-permute-start.11 = (f32[1,256,256]{2,1,0:T(8,128)S(1)}, f32[1,256,256]{2,1,0:T(8,128)S(1)}, u32[]{:S(2)}, u32[]{:S(2)}) collective-permute-start(f32[1,256,256]{2,1,0:T(8,128)S(1)} %fusion.6), channel_id=1, source_target_pairs={{0,16},{1,9},{2,18},{3,11},{4,20},{5,13},{6,22},{7,15},{8,24},{9,1... | collective-permute-start | bytes 786440 | tf_op jit(solution)/shard_map/ppermute | solution.py:265
  86.1 9.4 %collective-permute-start.13 = (f32[1,128,256]{2,1,0:T(8,128)S(1)}, f32[1,128,256]{2,1,0:T(8,128)S(1)}, u32[]{:S(2)}, u32[]{:S(2)}) collective-permute-start(f32[1,128,256]{2,1,0:T(8,128)S(1)} %slice.195), channel_id=1, source_target_pairs={{0,2},{1,3},{2,0},{3,1},{4,6},{5,7},{6,4},{7,5},{8,10},{9,11},{10,... | collective-permute-start | bytes 393224 | tf_op jit(solution)/shard_map/ppermute | solution.py:247
  89.6 27.9 %collective-permute-start.12 = (f32[2,256,512]{2,1,0:T(8,128)S(1)}, f32[2,256,512]{2,1,0:T(8,128)S(1)}, u32[]{:S(2)}, u32[]{:S(2)}) collective-permute-start(f32[2,256,512]{2,1,0:T(8,128)S(1)} %add_add_fusion), channel_id=1, source_target_pairs={{0,8},{8,16},{16,24},{1,9},{9,17},{17,25},{2,10},{10,18},{18,26},{... | collective-permute-start | bytes 3145736 | tf_op jit(solution)/shard_map/ppermute | solution.py:18
  94.3 6.4 %collective-permute-start.18 = (f32[1,128,256]{2,1,0:T(8,128)S(1)}, f32[1,128,256]{2,1,0:T(8,128)S(1)}, u32[]{:S(2)}, u32[]{:S(2)}) collective-permute-start(f32[1,128,256]{2,1,0:T(8,128)S(1)} %slice.200), channel_id=1, source_target_pairs={{0,2},{1,3},{2,0},{3,1},{4,6},{5,7},{6,4},{7,5},{8,10},{9,11},{10,... | collective-permute-start | bytes 393224 | tf_op jit(solution)/shard_map/ppermute | solution.py:247
  95.5 10.7 %collective-permute-start.14 = (f32[1,128,256]{2,1,0:T(8,128)S(1)}, f32[1,128,256]{2,1,0:T(8,128)S(1)}, u32[]{:S(2)}, u32[]{:S(2)}) collective-permute-start(f32[1,128,256]{2,1,0:T(8,128)S(1)} %slice_add_fusion.12), channel_id=1, source_target_pairs={{0,4},{1,5},{2,6},{3,7},{4,0},{5,1},{6,2},{7,3},{8,12},{9,13},{10,... | collective-permute-start | bytes 393224 | tf_op jit(solution)/shard_map/ppermute | solution.py:247
  100.8 8.3 %collective-permute-start.19 = (f32[1,128,256]{2,1,0:T(8,128)S(1)}, f32[1,128,256]{2,1,0:T(8,128)S(1)}, u32[]{:S(2)}, u32[]{:S(2)}) collective-permute-start(f32[1,128,256]{2,1,0:T(8,128)S(1)} %slice_add_fusion.11), channel_id=1, source_target_pairs={{0,4},{1,5},{2,6},{3,7},{4,0},{5,1},{6,2},{7,3},{8,12},{9,13},{10,... | collective-permute-start | bytes 393224 | tf_op jit(solution)/shard_map/ppermute | solution.py:247
  106.2 5.8 %collective-permute-start.15 = (f32[1,128,256]{2,1,0:T(8,128)S(1)}, f32[1,128,256]{2,1,0:T(8,128)S(1)}, u32[]{:S(2)}, u32[]{:S(2)}) collective-permute-start(f32[1,128,256]{2,1,0:T(8,128)S(1)} %add.212), channel_id=1, source_target_pairs={{0,2},{1,3},{2,0},{3,1},{4,6},{5,7},{6,4},{7,5},{8,10},{9,11},{10,... | collective-permute-start | bytes 393224 | tf_op jit(solution)/shard_map/ppermute | solution.py:247
  109.1 10.0 %collective-permute-start.20 = (f32[1,128,256]{2,1,0:T(8,128)S(1)}, f32[1,128,256]{2,1,0:T(8,128)S(1)}, u32[]{:S(2)}, u32[]{:S(2)}) collective-permute-start(f32[1,128,256]{2,1,0:T(8,128)S(1)} %add.220), channel_id=1, source_target_pairs={{0,2},{1,3},{2,0},{3,1},{4,6},{5,7},{6,4},{7,5},{8,10},{9,11},{10,... | collective-permute-start | bytes 393224 | tf_op jit(solution)/shard_map/ppermute | solution.py:247
  112.1 9.6 %collective-permute-start.16 = (f32[1,256,256]{2,1,0:T(8,128)S(1)}, f32[1,256,256]{2,1,0:T(8,128)S(1)}, u32[]{:S(2)}, u32[]{:S(2)}) collective-permute-start(f32[1,256,256]{2,1,0:T(8,128)S(1)} %get-tuple-element.57), channel_id=1, source_target_pairs={{0,16},{1,9},{2,18},{3,11},{4,20},{5,13},{6,22},{7,15},{8,24},{9,1... | collective-permute-start | bytes 786440 | tf_op jit(solution)/shard_map/ppermute | solution.py:265
  119.1 9.7 %collective-permute-start.21 = (f32[1,256,256]{2,1,0:T(8,128)S(1)}, f32[1,256,256]{2,1,0:T(8,128)S(1)}, u32[]{:S(2)}, u32[]{:S(2)}) collective-permute-start(f32[1,256,256]{2,1,0:T(8,128)S(1)} %maximum_add_fusion.1), channel_id=1, source_target_pairs={{0,16},{1,9},{2,18},{3,11},{4,20},{5,13},{6,22},{7,15},{8,24},{9,1... | collective-permute-start | bytes 786440 | tf_op jit(solution)/shard_map/ppermute | solution.py:265
  121.7 9.3 %collective-permute-start.17 = (f32[1,2,256,256]{3,2,1,0:T(8,128)S(1)}, f32[1,2,256,256]{3,2,1,0:T(8,128)S(1)}, u32[]{:S(2)}, u32[]{:S(2)}) collective-permute-start(f32[1,2,256,256]{3,2,1,0:T(8,128)S(1)} %pad_maximum_fusion.refs_0_), channel_id=1, source_target_pairs={{0,8},{1,17},{2,10},{3,19},{4,12},{5,21},{6,14},{7,23},{8,0},{9,25... | collective-permute-start | bytes 1572872 | tf_op jit(solution)/shard_map/ppermute | solution.py:265
  128.9 9.3 %collective-permute-start.22 = (f32[1,2,256,256]{3,2,1,0:T(8,128)S(1)}, f32[1,2,256,256]{3,2,1,0:T(8,128)S(1)}, u32[]{:S(2)}, u32[]{:S(2)}) collective-permute-start(f32[1,2,256,256]{3,2,1,0:T(8,128)S(1)} %pad_maximum_fusion.1.refs_2_), channel_id=1, source_target_pairs={{0,8},{1,17},{2,10},{3,19},{4,12},{5,21},{6,14},{7,23},{8,0},{9,25... | collective-permute-start | bytes 1572872 | tf_op jit(solution)/shard_map/ppermute | solution.py:265
  131.0 7.7 %collective-permute-start.23 = (f32[1,2,256,256]{3,2,1,0:T(8,128)S(1)}, f32[1,2,256,256]{3,2,1,0:T(8,128)S(1)}, u32[]{:S(2)}, u32[]{:S(2)}) collective-permute-start(f32[1,2,256,256]{3,2,1,0:T(8,128)S(1)} %pad_maximum_fusion.refs_0_), channel_id=1, source_target_pairs={{0,1},{1,0},{2,3},{3,2},{4,5},{5,4},{6,7},{7,6},{8,9},{9,8},{10,11... | collective-permute-start | bytes 1572872 | tf_op jit(solution)/shard_map/ppermute | solution.py:247
  131.0 7.7 %collective-permute-start.24 = (f32[1,2,256,256]{3,2,1,0:T(8,128)S(1)}, f32[1,2,256,256]{3,2,1,0:T(8,128)S(1)}, u32[]{:S(2)}, u32[]{:S(2)}) collective-permute-start(f32[1,2,256,256]{3,2,1,0:T(8,128)S(1)} %collective-permute-done.17.refs_1_), channel_id=1, source_target_pairs={{0,1},{1,0},{2,3},{3,2},{4,5},{5,4},{6,7},{7,6},{8,9},{9,8},{10,11... | collective-permute-start | bytes 1572872 | tf_op jit(solution)/shard_map/ppermute | solution.py:247
  131.5 7.3 %collective-permute-start.25 = (f32[1,2,256,256]{3,2,1,0:T(8,128)S(1)}, f32[1,2,256,256]{3,2,1,0:T(8,128)S(1)}, u32[]{:S(2)}, u32[]{:S(2)}) collective-permute-start(f32[1,2,256,256]{3,2,1,0:T(8,128)S(1)} %pad_maximum_fusion.1.refs_2_), channel_id=1, source_target_pairs={{0,1},{1,0},{2,3},{3,2},{4,5},{5,4},{6,7},{7,6},{8,9},{9,8},{10,11... | collective-permute-start | bytes 1572872 | tf_op jit(solution)/shard_map/ppermute | solution.py:247
  (11 other events, 140.6 us)
